TPU v7x, 128 devices: a whole 4x4x4 slice. The times are simulated.
128 devices in a mesh: gx: 16 (over z, y), gy: 8 (over x, core).
Axes of the slice: x: 4, y: 4, z: 4, core: 2. Of those that a mesh axis runs over, the one named last changes fastest.
Arguments:
- fields: float32 [4, 1, 2048, 2048], P(None, None, 'gx', 'gy'), may hold values from -1200 to 1200
- viscosity: float32 [1, 2048, 2048], P(None, 'gx', 'gy'), may hold values from 0.25 to 4
- diffusivity: float32 [1, 2048, 2048], P(None, 'gx', 'gy'), may hold values from 0.25 to 4
Outputs:
- updated: float32 [4, 1, 2048, 2048], P(None, None, 'gx', 'gy')
All inputs are finite; a program needn't handle non-finite values.
Results may differ from a plain program's by a relative error of at most 0.0003.
Values sent between devices are 32-bit elements; how exact they have to be, the bound alone decides.
No kernel may reach another device: no remote copies, remote signals or barrier semaphores. Data moves between devices by JAX's collectives and lax.ppermute only.
A program may use at most 64 MiB of HBM per device.

v0:
```python
import functools

import jax
import jax.numpy as jnp
from jax import lax
from jax.experimental import pallas as pl
from jax.experimental.pallas import tpu as pltpu
from jax.sharding import PartitionSpec as P


FIELDS = 4
KIND = (0, 0, 0, 1)
LANES = 128
SUB = 8
COEF_ROWS = 5
QUANTITIES = 2 * COEF_ROWS + 2 * FIELDS


def recip(value):
    guess = pl.reciprocal(value, approx=True)
    return guess * (2.0 - value * guess)


def up(rows, step):
    step %= rows.shape[0]
    return pltpu.roll(rows, rows.shape[0] - step, 0) if step else rows


def down(rows, step):
    return pltpu.roll(rows, step, 0)


def row_index(rows):
    return lax.broadcasted_iota(jnp.int32, (rows, LANES), 0)


def pair(left, ground_u, link, ground_v, right):
    total_u, total_v = left + ground_u, right + ground_v
    scale = recip(total_u * total_v + link * (total_u + total_v))
    return (total_v + link) * scale, link * scale, (total_u + link) * scale


def join(link, ground_a, ground_b, face, shift):
    right, ground_v = up(link, shift), up(ground_a, shift)
    uu, uv, vv = pair(link, ground_b, face, ground_v, right)
    u_left, v_left, u_right, v_right = link * uu, link * uv, right * uv, right * vv
    joined = (
        v_left * right,
        ground_a + ground_b * u_left + ground_v * v_left,
        up(ground_b, shift) + ground_b * u_right + ground_v * v_right,
    )
    return joined, (uu, uv, vv, u_left, v_left, u_right, v_right)


def join_sources(source_a, source_b, weights, shift):
    _, _, _, u_left, v_left, u_right, v_right = weights
    source_v = up(source_a, shift)
    return (
        source_a + source_b * u_left + source_v * v_left,
        up(source_b, shift) + source_b * u_right + source_v * v_right,
    )


def eliminate(coefs, half):
    count = len(coefs)
    ground = [1.0] * count
    links = [half * (coefs[i] + coefs[i + 1]) for i in range(count - 1)]
    nodes, plan = list(range(count)), []
    while len(nodes) > 2:
        kept, kept_links, i = [nodes[0]], [], 1
        while i <= len(nodes) - 2:
            low, cell, high = kept[-1], nodes[i], nodes[i + 1]
            scale = recip(links[i - 1] + links[i] + ground[cell])
            to_low, to_high = links[i - 1] * scale, links[i] * scale
            ground[low] = ground[low] + to_low * ground[cell]
            ground[high] = ground[high] + to_high * ground[cell]
            kept.append(high)
            kept_links.append(to_low * links[i])
            plan.append((cell, low, high, scale, to_low, to_high))
            i += 2
        if i == len(nodes) - 1:
            kept.append(nodes[i])
            kept_links.append(links[i - 1])
        nodes, links = kept, kept_links
    face = half * (coefs[-1] + up(coefs[0], 1))
    chain, joins = (links[0], ground[0], ground[-1]), []
    for shift in (1, 2, 4):
        chain, weights = join(*chain, up(face, shift - 1), shift)
        joins.append((shift, weights))
    return plan, joins, chain


def push_sources(plan, joins, sources):
    sources = list(sources)
    for cell, low, high, _, to_low, to_high in plan:
        sources[low] = sources[low] + to_low * sources[cell]
        sources[high] = sources[high] + to_high * sources[cell]
    ends, history = (sources[0], sources[-1]), []
    for shift, weights in joins:
        history.append(ends)
        ends = join_sources(*ends, weights, shift)
    return sources, history, ends


def pull_values(plan, joins, count, end_a, end_b, sources=None, history=None):
    row = row_index(SUB)
    for index in reversed(range(len(joins))):
        shift, (uu, uv, vv, u_left, v_left, u_right, v_right) = joins[index]
        value_u = u_left * end_a + u_right * end_b
        value_v = v_left * end_a + v_right * end_b
        if history is not None:
            source_u, source_v = history[index][1], up(history[index][0], shift)
            value_u = value_u + uu * source_u + uv * source_v
            value_v = value_v + uv * source_u + vv * source_v
        on_right = (row // shift) % 2 == 1
        end_a = jnp.where(on_right, down(value_v, shift), end_a)
        end_b = jnp.where(on_right, down(end_b, shift), value_u)
    values = [None] * count
    values[0], values[-1] = end_a, end_b
    for cell, low, high, scale, to_low, to_high in reversed(plan):
        value = to_low * values[low] + to_high * values[high]
        values[cell] = value if sources is None else value + scale * sources[cell]
    return values


def responses(plan, joins, count):
    one = jnp.ones((SUB, LANES), jnp.float32)
    zero = jnp.zeros((SUB, LANES), jnp.float32)
    return (
        pull_values(plan, joins, count, one, zero),
        pull_values(plan, joins, count, zero, one),
    )


def inside(plan, joins, count, sources):
    zero = jnp.zeros((SUB, LANES), jnp.float32)
    pushed, history, _ = push_sources(plan, joins, sources)
    return pull_values(plan, joins, count, zero, zero, pushed, history)


def load_cells(ref, count):
    return [ref[pl.ds(t, SUB, stride=count), :] for t in range(count)]


def store_cells(ref, values):
    for t, value in enumerate(values):
        ref[pl.ds(t, SUB, stride=len(values)), :] = value


def tiles(array):
    x_cells, y_cells = array.shape[-2:]
    split = array.reshape(-1, x_cells // SUB, SUB, y_cells // LANES, LANES)
    return split.transpose(0, 1, 3, 2, 4).reshape(-1, LANES)


def untiles(flat, shape):
    split = flat.reshape(-1, shape[-2] // SUB, shape[-1] // LANES, SUB, LANES)
    return split.transpose(0, 1, 3, 2, 4).reshape(shape)


def tile_at(field, x_tile, block, x_cells, blocks):
    return ((field * (x_cells // SUB) + x_tile) * blocks + block) * SUB


def load_x_cells(ref, field, block, x_cells, blocks):
    count = x_cells // SUB
    return [
        ref[pl.ds(tile_at(field, t // SUB, block, x_cells, blocks) + t % SUB, SUB, stride=count * blocks), :]
        for t in range(count)
    ]


def load_block(ref, field, block, x_cells, blocks):
    return jnp.concatenate(
        [ref[pl.ds(tile_at(field, i, block, x_cells, blocks), SUB), :] for i in range(x_cells // SUB)]
    )


def load_turned(ref, field, x_cells, blocks, turned):
    for block in range(blocks):
        turned[pl.ds(block * LANES, LANES), :] = load_block(ref, field, block, x_cells, blocks).T


def solve_ring(quantity, ranks, rank, half):
    row = row_index(ranks)
    device = lax.rem(row + (rank + 1), ranks)
    first, last = device == 0, device == ranks - 1
    results = []
    for kind in range(2):
        first_coef, last_coef, link, ground_a, ground_b = [
            quantity(kind * COEF_ROWS + i) for i in range(COEF_ROWS)
        ]
        ground_a = ground_a + jnp.where(first, half * first_coef, 0.0)
        ground_b = ground_b + jnp.where(last, half * last_coef, 0.0)
        face = jnp.where(last, 0.0, half * (last_coef + up(first_coef, 1)))
        own = [up(x, ranks - 1) for x in (link, ground_a, ground_b)]
        left, right = up(face, ranks - 1), up(face, ranks - 2)
        fields = [f for f in range(FIELDS) if KIND[f] == kind]
        sources = [
            (quantity(2 * COEF_ROWS + 2 * f), quantity(2 * COEF_ROWS + 2 * f + 1)) for f in fields
        ]
        own_sources = [[up(x, ranks - 1) for x in pair_] for pair_ in sources]
        chain, shift = (link, ground_a, ground_b), 1
        while shift < ranks:
            joined, weights = join(*chain, up(face, shift - 1), shift)
            joined_sources = [join_sources(*s, weights, shift) for s in sources]
            if shift == 1:
                alone = row == ranks - 2
                joined = [jnp.where(alone, a, b) for a, b in zip(chain, joined)]
                joined_sources = [
                    [jnp.where(alone, a, b) for a, b in zip(old, new)]
                    for old, new in zip(sources, joined_sources)
                ]
            chain, sources, shift = joined, joined_sources, 2 * shift
        link, ground_u, ground_v = chain
        uu, uv, vv = pair(left, ground_u, link, ground_v, right)
        u_b, v_b, u_a, v_a = left * uu, left * uv, right * uv, right * vv
        link = own[0] + v_b * right
        ground_a = own[1] + ground_u * u_a + ground_v * v_a
        ground_b = own[2] + ground_u * u_b + ground_v * v_b
        scale = recip(ground_a * ground_b + link * (ground_a + ground_b))
        aa, ab, bb = (ground_b + link) * scale, link * scale, (ground_a + link) * scale
        for (source_u, source_v), (source_a, source_b) in zip(sources, own_sources):
            source_a = source_a + source_u * u_a + source_v * v_a
            source_b = source_b + source_u * u_b + source_v * v_b
            results.append((aa * source_a + ab * source_b, ab * source_a + bb * source_b))
    return results


def rotate(received, turned, ranks, rows, rank):
    for k in range(ranks):
        source = pl.multiple_of(lax.rem(rank + 1 + k, ranks) * rows, SUB)
        turned[pl.ds(k * rows, rows), :] = received[pl.ds(source, rows), :]


def coef_rows(coefs, chain):
    return (coefs[0][:1], coefs[-1][SUB - 1 :], chain[0][:1], chain[1][:1], chain[2][:1])


def x_ends_kernel(half, x_cells, blocks, ranks, rows, fields, viscosity, diffusivity, message, line):
    line[...] = jnp.zeros_like(line)
    for block in range(blocks):

        def put(quantity, value):
            at = quantity * blocks + block
            line[at : at + 1, :] = value

        for kind, coef in enumerate((viscosity, diffusivity)):
            coefs = load_x_cells(coef, 0, block, x_cells, blocks)
            plan, joins, chain = eliminate(coefs, half)
            for i, value in enumerate(coef_rows(coefs, chain)):
                put(kind * COEF_ROWS + i, value)
            for f in range(FIELDS):
                if KIND[f] == kind:
                    _, _, ends = push_sources(plan, joins, load_x_cells(fields, f, block, x_cells, blocks))
                    put(2 * COEF_ROWS + 2 * f, ends[0][:1])
                    put(2 * COEF_ROWS + 2 * f + 1, ends[1][:1])
    for k in range(ranks):
        message[pl.ds(k * rows, rows), :] = line[...]


def local_kernel(
    half_x, half_y, x_cells, blocks,
    fields, viscosity, diffusivity, inner, x_a, x_b, y_a, y_b, y_rows, turned, result,
):
    count, y_count = x_cells // SUB, blocks * LANES // SUB
    y_rows[...] = jnp.zeros_like(y_rows)
    for kind, coef in enumerate((viscosity, diffusivity)):
        for block in range(blocks):
            plan, joins, _ = eliminate(load_x_cells(coef, 0, block, x_cells, blocks), half_x)
            from_a, from_b = responses(plan, joins, count)
            store_cells(x_a.at[kind, block], from_a)
            store_cells(x_b.at[kind, block], from_b)
            for f in range(FIELDS):
                if KIND[f] == kind:
                    sources = load_x_cells(fields, f, block, x_cells, blocks)
                    store_cells(inner.at[f, block], inside(plan, joins, count, sources))
        load_turned(coef, 0, x_cells, blocks, turned)
        coefs = load_cells(turned, y_count)
        plan, joins, chain = eliminate(coefs, half_y)
        for i, value in enumerate(coef_rows(coefs, chain)):
            y_rows[kind * COEF_ROWS + i : kind * COEF_ROWS + i + 1, :] = value
        for out, values in zip((y_a, y_b), responses(plan, joins, y_count)):
            store_cells(result, values)
            for block in range(blocks):
                out[kind, block] = result[pl.ds(block * LANES, LANES), :].T


def x_join_kernel(
    half, axis, ranks, rows, y_ranks, y_rows_count,
    received, inner, x_a, x_b, y_a, y_b, y_rows, swept, message, turned, line,
):
    blocks, x_cells = inner.shape[1:3]
    rank = lax.axis_index(axis)
    rotate(received, turned, ranks, rows, rank)
    for block in range(blocks):
        ends = solve_ring(
            lambda q: turned[pl.ds(q * blocks + block, ranks, stride=rows), :], ranks, rank, half
        )
        for f in range(FIELDS):
            end_a, end_b = ends[f]
            swept[f, block] = inner[f, block] + x_a[KIND[f], block] * end_a[:1] + x_b[KIND[f], block] * end_b[:1]
    line[...] = y_rows[...]
    diagonal = row_index(x_cells) == lax.broadcasted_iota(jnp.int32, (x_cells, LANES), 1)
    for f in range(FIELDS):
        for end, weights in enumerate((y_a, y_b)):
            total = sum(weights[KIND[f], block] * swept[f, block] for block in range(blocks))
            sums = jnp.sum(total, axis=1, keepdims=True)
            at = 2 * COEF_ROWS + 2 * f + end
            line[at : at + 1, :] = jnp.sum(jnp.where(diagonal, sums, 0.0), axis=0, keepdims=True)
    for k in range(y_ranks):
        message[pl.ds(k * y_rows_count, y_rows_count), :] = line[...]


def y_inside_kernel(half, swept, viscosity, diffusivity, inner, turned, result):
    blocks, x_cells = swept.shape[1:3]
    count = blocks * LANES // SUB
    for kind, coef in enumerate((viscosity, diffusivity)):
        load_turned(coef, 0, x_cells, blocks, turned)
        plan, joins, _ = eliminate(load_cells(turned, count), half)
        for f in range(FIELDS):
            if KIND[f] == kind:
                for block in range(blocks):
                    turned[pl.ds(block * LANES, LANES), :] = swept[f, block].T
                store_cells(result, inside(plan, joins, count, load_cells(turned, count)))
                for block in range(blocks):
                    inner[f, block] = result[pl.ds(block * LANES, LANES), :].T


def y_join_kernel(half, axis, ranks, rows, received, inner, y_a, y_b, updated, turned):
    blocks, x_cells = inner.shape[1:3]
    rank = lax.axis_index(axis)
    rotate(received, turned, ranks, rows, rank)
    ends = solve_ring(lambda q: turned[pl.ds(q, ranks, stride=rows), :], ranks, rank, half)
    for f in range(FIELDS):
        end_a, end_b = [jnp.broadcast_to(e[:1], (x_cells, LANES)).T for e in ends[f]]
        for block in range(blocks):
            value = inner[f, block] + y_a[KIND[f], block] * end_a + y_b[KIND[f], block] * end_b
            for i in range(x_cells // SUB):
                updated[pl.ds(tile_at(f, i, block, x_cells, blocks), SUB), :] = value[i * SUB : (i + 1) * SUB]


def call(kernel, outs, scratch, name):
    return pl.pallas_call(
        kernel,
        out_shape=[jax.ShapeDtypeStruct(s, jnp.float32) for s in outs],
        scratch_shapes=[pltpu.VMEM(s, jnp.float32) for s in scratch],
        compiler_params=pltpu.CompilerParams(vmem_limit_bytes=24 * 1024 * 1024),
        name=name,
    )


def padded(rows):
    return -(-rows // SUB) * SUB


def on_device(x_ranks, y_ranks, fields, viscosity, diffusivity):
    _, _, x_cells, y_cells = fields.shape
    blocks = y_cells // LANES
    half_x, half_y = 0.5 * float(x_cells * x_cells), 0.5 * float(y_cells * y_cells)
    x_rows, y_rows = padded(QUANTITIES * blocks), padded(QUANTITIES)
    block, pairs, turned = (FIELDS, blocks, x_cells, LANES), (2, blocks, x_cells, LANES), (y_cells, x_cells)
    args = [tiles(a) for a in (fields, viscosity, diffusivity)]

    (message,) = call(
        functools.partial(x_ends_kernel, half_x, x_cells, blocks, x_ranks, x_rows),
        [(x_ranks * x_rows, LANES)], [(x_rows, LANES)], "x_ends",
    )(*args)
    received = lax.all_to_all(message.reshape(x_ranks, x_rows, LANES), "gx", 0, 0, tiled=True)
    inner, x_a, x_b, y_a, y_b, y_coefs = call(
        functools.partial(local_kernel, half_x, half_y, x_cells, blocks),
        [block, pairs, pairs, pairs, pairs, (y_rows, LANES)], [turned, turned], "local",
    )(*args)
    swept, message = call(
        functools.partial(x_join_kernel, half_x, "gx", x_ranks, x_rows, y_ranks, y_rows),
        [block, (y_ranks * y_rows, LANES)],
        [(x_ranks * x_rows, LANES), (y_rows, LANES)], "x_join",
    )(received.reshape(x_ranks * x_rows, LANES), inner, x_a, x_b, y_a, y_b, y_coefs)
    received = lax.all_to_all(message.reshape(y_ranks, y_rows, LANES), "gy", 0, 0, tiled=True)
    (inner,) = call(functools.partial(y_inside_kernel, half_y), [block], [turned, turned], "y_inside")(swept, *args[1:])
    (updated,) = call(
        functools.partial(y_join_kernel, half_y, "gy", y_ranks, y_rows),
        [(FIELDS * x_cells * blocks, LANES)], [(y_ranks * y_rows, LANES)], "y_join",
    )(received.reshape(y_ranks * y_rows, LANES), inner, y_a, y_b)
    return untiles(updated, fields.shape)


def solution(mesh):
    placed = (P(None, None, "gx", "gy"), P(None, "gx", "gy"), P(None, "gx", "gy"))
    return jax.shard_map(
        functools.partial(on_device, mesh.shape["gx"], mesh.shape["gy"]),
        mesh=mesh, in_specs=placed, out_specs=P(None, None, "gx", "gy"), check_vma=False,
    )
```

profile of v0, /device:TPU:1, one launch (start us, length us, event | category | flops | bytes accessed | tf_op | source)
XLA Modules:
  0.0 35.0 jit_solution(5943037684047478274)
XLA Ops:
  0.0 0.0 copy-start
  0.0 1.0 %copy-done = f32[4,1,128,256]{3,2,1,0:T(8,128)S(1)} copy-done((f32[4,1,128,256]{3,2,1,0:T(8,128)S(1)}, f32[4,1,128,256]{3,2,1,0:T(8,128)}, u32[]{:S(2)}) %copy-start) | copy-done | bytes 524312
  1.0 0.0 copy-start.2
  1.0 0.9 %copy-done.2 = f32[1,128,256]{2,1,0:T(8,128)S(1)} copy-done((f32[1,128,256]{2,1,0:T(8,128)S(1)}, f32[1,128,256]{2,1,0:T(8,128)}, u32[]{:S(2)}) %copy-start.2) | copy-done | bytes 131096
  1.9 0.0 copy-start.4
  1.9 0.9 %copy-done.4 = f32[1,128,256]{2,1,0:T(8,128)S(1)} copy-done((f32[1,128,256]{2,1,0:T(8,128)S(1)}, f32[1,128,256]{2,1,0:T(8,128)}, u32[]{:S(2)}) %copy-start.4) | copy-done | bytes 131096
  2.9 0.0 copy-start.5
  2.9 1.4 %x_ends.1 = f32[640,128]{1,0:T(8,128)} custom-call(f32[1024,128]{1,0:T(8,128)S(1)} %bitcast.24, f32[256,128]{1,0:T(8,128)S(1)} %bitcast.27, f32[256,128]{1,0:T(8,128)S(1)} %bitcast.30), custom_call_target="tpu_custom_call" | custom-call | tf_op jit(solution)/shard_map/x_ends/pallas_call | solution.py:365
  4.2 0.0 copy-start.1
  4.2 0.0 copy-start.3
  4.2 8.7 %all-to-all-start = ((f32[16,40,128]{2,1,0:T(8,128)}), f32[16,40,128]{2,1,0:T(8,128)S(1)}, u32[]{:S(2)}, u32[]{:S(2)}) async-start(f32[16,40,128]{2,1,0:T(8,128)} %bitcast.9), calls=%async_computation | async-start | bytes 655360 | tf_op jit(solution)/shard_map/all_to_all | solution.py:369
  13.0 0.0 copy-done.5
  13.0 0.0 copy-done.1
  13.0 0.0 copy-done.3
  13.0 1.9 %local.1 = (f32[4,2,128,128]{3,2,1,0:T(8,128)S(1)}, f32[2,2,128,128]{3,2,1,0:T(8,128)S(1)}, f32[2,2,128,128]{3,2,1,0:T(8,128)S(1)}, f32[2,2,128,128]{3,2,1,0:T(8...) custom-call(f32[1024,128]{1,0:T(8,128)S(1)} %bitcast.25, f32[256,128]{1,0:T(8,128)S(1)} %bitcast.28, ...), custom_call_target="tpu_custom_call" | custom-call | tf_op jit(solution)/shard_map/local/pallas_call | solution.py:370
  14.9 6.6 %all-to-all-done = f32[16,40,128]{2,1,0:T(8,128)S(1)} async-done(((f32[16,40,128]{2,1,0:T(8,128)}), f32[16,40,128]{2,1,0:T(8,128)S(1)}, u32[]{:S(2)}, u32[]{:S(2)}) %all-to-all-start) | async-done | bytes 327712 | tf_op jit(solution)/shard_map/all_to_all | solution.py:369
  21.4 1.3 %x_join.1 = (f32[4,2,128,128]{3,2,1,0:T(8,128)S(1)}, f32[192,128]{1,0:T(8,128)}) custom-call(f32[640,128]{1,0:T(8,128)S(1)} %bitcast.26, f32[4,2,128,128]{3,2,1,0:T(8,128)S(1)} %get-tuple-element.13.inner, f32[2,2,128,128]{3,2,1,0:T(8,128)S(1)} %get-tuple-element.14.x_a, f32[2,2,128,128]{3,2,1,0:T(8,128)S(1)} %get-tuple-element.15.x_b, ...), custom_call_target="tpu_custom_call" | custom-call | tf_op jit(solution)/shard_map/x_join/pallas_call | solution.py:374
  22.7 6.2 %all-to-all-start.1 = ((f32[8,24,128]{2,1,0:T(8,128)}), f32[8,24,128]{2,1,0:T(8,128)S(1)}, u32[]{:S(2)}, u32[]{:S(2)}) async-start(f32[8,24,128]{2,1,0:T(8,128)} %bitcast.17), calls=%async_computation.1 | async-start | bytes 196608 | tf_op jit(solution)/shard_map/all_to_all | solution.py:379
  28.9 1.5 %y_inside.1.inner = f32[4,2,128,128]{3,2,1,0:T(8,128)S(1)} custom-call(f32[4,2,128,128]{3,2,1,0:T(8,128)S(1)} %get-tuple-element.20.swept, f32[256,128]{1,0:T(8,128)S(1)} %bitcast.29, f32[256,128]{1,0:T(8,128)S(1)} %bitcast.32), custom_call_target="tpu_custom_call" | custom-call | tf_op jit(solution)/shard_map/y_inside/pallas_call | solution.py:380
  30.4 3.5 %all-to-all-done.1 = f32[8,24,128]{2,1,0:T(8,128)S(1)} async-done(((f32[8,24,128]{2,1,0:T(8,128)}), f32[8,24,128]{2,1,0:T(8,128)S(1)}, u32[]{:S(2)}, u32[]{:S(2)}) %all-to-all-start.1) | async-done | bytes 98336 | tf_op jit(solution)/shard_map/all_to_all | solution.py:379
  33.9 1.1 %y_join.1 = f32[1024,128]{1,0:T(8,128)} custom-call(f32[192,128]{1,0:T(8,128)S(1)} %bitcast.33, f32[4,2,128,128]{3,2,1,0:T(8,128)S(1)} %y_inside.1.inner, f32[2,2,128,128]{3,2,1,0:T(8,128)S(1)} %get-tuple-element.16.y_a, f32[2,2,128,128]{3,2,1,0:T(8,128)S(1)} %get-tuple-element.17.y_b), custom_call_target="tpu_custom_call" | custom-call | tf_op jit(solution)/shard_map/y_join/pallas_call | solution.py:381
Async XLA Ops:
  0.0 1.0 %copy-start = (f32[4,1,128,256]{3,2,1,0:T(8,128)S(1)}, f32[4,1,128,256]{3,2,1,0:T(8,128)}, u32[]{:S(2)}) copy-start(f32[4,1,128,256]{3,2,1,0:T(8,128)} %param.3) | copy-start | bytes 1572868
  1.0 0.9 %copy-start.2 = (f32[1,128,256]{2,1,0:T(8,128)S(1)}, f32[1,128,256]{2,1,0:T(8,128)}, u32[]{:S(2)}) copy-start(f32[1,128,256]{2,1,0:T(8,128)} %param.4) | copy-start | bytes 393220
  1.9 0.9 %copy-start.4 = (f32[1,128,256]{2,1,0:T(8,128)S(1)}, f32[1,128,256]{2,1,0:T(8,128)}, u32[]{:S(2)}) copy-start(f32[1,128,256]{2,1,0:T(8,128)} %param.5) | copy-start | bytes 393220
  2.9 10.1 %copy-start.5 = (f32[1,128,256]{2,1,0:T(8,128)S(1)}, f32[1,128,256]{2,1,0:T(8,128)}, u32[]{:S(2)}) copy-start(f32[1,128,256]{2,1,0:T(8,128)} %param.5) | copy-start | bytes 393220
  4.2 8.8 %copy-start.1 = (f32[4,1,128,256]{3,2,1,0:T(8,128)S(1)}, f32[4,1,128,256]{3,2,1,0:T(8,128)}, u32[]{:S(2)}) copy-start(f32[4,1,128,256]{3,2,1,0:T(8,128)} %param.3) | copy-start | bytes 1572868
  4.2 8.8 %copy-start.3 = (f32[1,128,256]{2,1,0:T(8,128)S(1)}, f32[1,128,256]{2,1,0:T(8,128)}, u32[]{:S(2)}) copy-start(f32[1,128,256]{2,1,0:T(8,128)} %param.4) | copy-start | bytes 393220
  4.2 17.2 %all-to-all-start = ((f32[16,40,128]{2,1,0:T(8,128)}), f32[16,40,128]{2,1,0:T(8,128)S(1)}, u32[]{:S(2)}, u32[]{:S(2)}) async-start(f32[16,40,128]{2,1,0:T(8,128)} %bitcast.9), calls=%async_computation | async-start | bytes 655360 | tf_op jit(solution)/shard_map/all_to_all | solution.py:369
  22.7 11.1 %all-to-all-start.1 = ((f32[8,24,128]{2,1,0:T(8,128)}), f32[8,24,128]{2,1,0:T(8,128)S(1)}, u32[]{:S(2)}, u32[]{:S(2)}) async-start(f32[8,24,128]{2,1,0:T(8,128)} %bitcast.17), calls=%async_computation.1 | async-start | bytes 196608 | tf_op jit(solution)/shard_map/all_to_all | solution.py:379
where the time goes:
time: 35.3 us; the launch traced here: 35 us
  starting transfers between devices  14.9 us (42%)
  waiting for transfers between devices  10.1 us (29%)
  Pallas kernels  7.11 us (20%)
  local copies, waits for them, and re-layouts  2.86 us (8%)
    all_to_all x1, starting transfers between devices, on_device(): lax.all_to_all(message.reshape(x_ranks, x_rows, LANES), 'gx', 0, 0, tiled...  8.73 us
    all_to_all x1, waiting for transfers between devices, on_device(): lax.all_to_all(message.reshape(x_ranks, x_rows, LANES), 'gx', 0, 0, tiled...  6.57 us
    all_to_all x1, starting transfers between devices, on_device(): lax.all_to_all(message.reshape(y_ranks, y_rows, LANES), 'gy', 0, 0, tiled...  6.16 us
    all_to_all x1, waiting for transfers between devices, on_device(): lax.all_to_all(message.reshape(y_ranks, y_rows, LANES), 'gy', 0, 0, tiled...  3.49 us
    unnamed x12, local copies, waits for them, and re-layouts  2.86 us
    pallas_call x1, Pallas kernels, on_device(): call(functools.partial(local_kernel, half_x, half_y, x_cells, blocks), [b...  1.87 us
    pallas_call x1, Pallas kernels, on_device(): call(functools.partial(y_inside_kernel, half_y), [block], [turned, turned...  1.48 us
    pallas_call x1, Pallas kernels, on_device(): call(functools.partial(x_ends_kernel, half_x, x_cells, blocks, x_ranks, x...  1.36 us
  transfers between devices with their start and end apart: 2, of which 2 were waited for; matrix products, arithmetic and copies ran while one was open for 0% of the time, Pallas kernels for 10%

commit v1 on v0

--- a/solution.py
+++ b/solution.py
@@ -237,24 +237,42 @@
     return (coefs[0][:1], coefs[-1][SUB - 1 :], chain[0][:1], chain[1][:1], chain[2][:1])
 
 
-def x_ends_kernel(half, x_cells, blocks, ranks, rows, fields, viscosity, diffusivity, message, line):
+def x_ends_kernel(
+    half, x_cells, blocks, ranks, rows,
+    fields, viscosity, diffusivity, message, line, fields_here, viscosity_here, diffusivity_here, arrived,
+):
+    per_field = x_cells * blocks
+    copies = [
+        pltpu.make_async_copy(viscosity, viscosity_here, arrived.at[0]),
+        pltpu.make_async_copy(diffusivity, diffusivity_here, arrived.at[1]),
+    ]
+    for f in range(FIELDS):
+        part = pl.ds(f * per_field, per_field)
+        copies.append(pltpu.make_async_copy(fields.at[part], fields_here.at[part], arrived.at[2 + f]))
+    for copy in copies:
+        copy.start()
     line[...] = jnp.zeros_like(line)
-    for block in range(blocks):
-
-        def put(quantity, value):
-            at = quantity * blocks + block
-            line[at : at + 1, :] = value
-
-        for kind, coef in enumerate((viscosity, diffusivity)):
+
+    def put(quantity, block, value):
+        at = quantity * blocks + block
+        line[at : at + 1, :] = value
+
+    plans = {}
+    for kind, coef in enumerate((viscosity_here, diffusivity_here)):
+        copies[kind].wait()
+        for block in range(blocks):
             coefs = load_x_cells(coef, 0, block, x_cells, blocks)
             plan, joins, chain = eliminate(coefs, half)
+            plans[kind, block] = plan, joins
             for i, value in enumerate(coef_rows(coefs, chain)):
-                put(kind * COEF_ROWS + i, value)
-            for f in range(FIELDS):
-                if KIND[f] == kind:
-                    _, _, ends = push_sources(plan, joins, load_x_cells(fields, f, block, x_cells, blocks))
-                    put(2 * COEF_ROWS + 2 * f, ends[0][:1])
-                    put(2 * COEF_ROWS + 2 * f + 1, ends[1][:1])
+                put(kind * COEF_ROWS + i, block, value)
+    for f in range(FIELDS):
+        copies[2 + f].wait()
+        for block in range(blocks):
+            sources = load_x_cells(fields_here, f, block, x_cells, blocks)
+            _, _, ends = push_sources(*plans[KIND[f], block], sources)
+            put(2 * COEF_ROWS + 2 * f, block, ends[0][:1])
+            put(2 * COEF_ROWS + 2 * f + 1, block, ends[1][:1])
     for k in range(ranks):
         message[pl.ds(k * rows, rows), :] = line[...]
 
@@ -327,27 +345,43 @@
                     inner[f, block] = result[pl.ds(block * LANES, LANES), :].T
 
 
-def y_join_kernel(half, axis, ranks, rows, received, inner, y_a, y_b, updated, turned):
+def y_join_kernel(half, axis, ranks, rows, received, inner, y_a, y_b, updated, turned, here, left):
     blocks, x_cells = inner.shape[1:3]
+    per_field = x_cells * blocks
     rank = lax.axis_index(axis)
     rotate(received, turned, ranks, rows, rank)
     ends = solve_ring(lambda q: turned[pl.ds(q, ranks, stride=rows), :], ranks, rank, half)
+    copies = []
     for f in range(FIELDS):
         end_a, end_b = [jnp.broadcast_to(e[:1], (x_cells, LANES)).T for e in ends[f]]
         for block in range(blocks):
             value = inner[f, block] + y_a[KIND[f], block] * end_a + y_b[KIND[f], block] * end_b
             for i in range(x_cells // SUB):
-                updated[pl.ds(tile_at(f, i, block, x_cells, blocks), SUB), :] = value[i * SUB : (i + 1) * SUB]
-
-
-def call(kernel, outs, scratch, name):
+                here[pl.ds(tile_at(f, i, block, x_cells, blocks), SUB), :] = value[i * SUB : (i + 1) * SUB]
+        part = pl.ds(f * per_field, per_field)
+        copies.append(pltpu.make_async_copy(here.at[part], updated.at[part], left.at[f]))
+        copies[-1].start()
+    for copy in copies:
+        copy.wait()
+
+
+def call(kernel, outs, scratch, name, **kw):
     return pl.pallas_call(
         kernel,
-        out_shape=[jax.ShapeDtypeStruct(s, jnp.float32) for s in outs],
-        scratch_shapes=[pltpu.VMEM(s, jnp.float32) for s in scratch],
+        out_shape=outs,
+        scratch_shapes=[pltpu.VMEM(s, jnp.float32) if isinstance(s, tuple) else s for s in scratch],
         compiler_params=pltpu.CompilerParams(vmem_limit_bytes=24 * 1024 * 1024),
         name=name,
-    )
+        **kw,
+    )
+
+
+def near(shape):
+    return pltpu.VMEM(shape, jnp.float32)
+
+
+def far(shape):
+    return pltpu.HBM(shape, jnp.float32)
 
 
 def padded(rows):
@@ -362,25 +396,34 @@
     block, pairs, turned = (FIELDS, blocks, x_cells, LANES), (2, blocks, x_cells, LANES), (y_cells, x_cells)
     args = [tiles(a) for a in (fields, viscosity, diffusivity)]
 
+    sizes = [a.shape for a in args]
+    in_hbm = [pltpu.with_memory_space_constraint(a, pltpu.HBM) for a in args]
+
     (message,) = call(
         functools.partial(x_ends_kernel, half_x, x_cells, blocks, x_ranks, x_rows),
-        [(x_ranks * x_rows, LANES)], [(x_rows, LANES)], "x_ends",
-    )(*args)
+        [near((x_ranks * x_rows, LANES))],
+        [(x_rows, LANES), *sizes, pltpu.SemaphoreType.DMA((2 + FIELDS,))], "x_ends",
+        in_specs=[pl.BlockSpec(memory_space=pltpu.HBM)] * 3,
+    )(*in_hbm)
     received = lax.all_to_all(message.reshape(x_ranks, x_rows, LANES), "gx", 0, 0, tiled=True)
     inner, x_a, x_b, y_a, y_b, y_coefs = call(
         functools.partial(local_kernel, half_x, half_y, x_cells, blocks),
-        [block, pairs, pairs, pairs, pairs, (y_rows, LANES)], [turned, turned], "local",
+        [near(s) for s in (block, pairs, pairs, pairs, pairs, (y_rows, LANES))], [turned, turned], "local",
     )(*args)
     swept, message = call(
         functools.partial(x_join_kernel, half_x, "gx", x_ranks, x_rows, y_ranks, y_rows),
-        [block, (y_ranks * y_rows, LANES)],
+        [near(block), near((y_ranks * y_rows, LANES))],
         [(x_ranks * x_rows, LANES), (y_rows, LANES)], "x_join",
     )(received.reshape(x_ranks * x_rows, LANES), inner, x_a, x_b, y_a, y_b, y_coefs)
     received = lax.all_to_all(message.reshape(y_ranks, y_rows, LANES), "gy", 0, 0, tiled=True)
-    (inner,) = call(functools.partial(y_inside_kernel, half_y), [block], [turned, turned], "y_inside")(swept, *args[1:])
+    (inner,) = call(
+        functools.partial(y_inside_kernel, half_y), [near(block)], [turned, turned], "y_inside"
+    )(swept, *args[1:])
     (updated,) = call(
         functools.partial(y_join_kernel, half_y, "gy", y_ranks, y_rows),
-        [(FIELDS * x_cells * blocks, LANES)], [(y_ranks * y_rows, LANES)], "y_join",
+        [far(sizes[0])],
+        [(y_ranks * y_rows, LANES), sizes[0], pltpu.SemaphoreType.DMA((FIELDS,))], "y_join",
+        out_specs=[pl.BlockSpec(memory_space=pltpu.HBM)],
     )(received.reshape(y_ranks * y_rows, LANES), inner, y_a, y_b)
     return untiles(updated, fields.shape)
 

time: 35.3 us -> 33.6 us (0.952)
  local copies, waits for them, and re-layouts: 2.86 us -> 0.02 us
  Pallas kernels: 7.11 us -> 8.21 us
    unnamed x12 -> x6, local copies, waits for them, and re-layouts: 2.86 us -> 0.02 us
    pallas_call x1, Pallas kernels: 1.36 us -> 2.53 us  [on_device(): call(functools.partial(x_ends_kernel, half_x, x_cells, blocks, x_ranks, x...]
where the time goes in v1:
time: 33.6 us; the launch traced here: 33.3 us
  starting transfers between devices  14.9 us (44%)
  waiting for transfers between devices  10.1 us (30%)
  Pallas kernels  8.21 us (24%)
    all_to_all x1, starting transfers between devices, on_device(): lax.all_to_all(message.reshape(x_ranks, x_rows, LANES), 'gx', 0, 0, tiled...  8.74 us
    all_to_all x1, waiting for transfers between devices, on_device(): lax.all_to_all(message.reshape(x_ranks, x_rows, LANES), 'gx', 0, 0, tiled...  6.57 us
    all_to_all x1, starting transfers between devices, on_device(): lax.all_to_all(message.reshape(y_ranks, y_rows, LANES), 'gy', 0, 0, tiled...  6.16 us
    all_to_all x1, waiting for transfers between devices, on_device(): lax.all_to_all(message.reshape(y_ranks, y_rows, LANES), 'gy', 0, 0, tiled...  3.49 us
    pallas_call x1, Pallas kernels, on_device(): call(functools.partial(x_ends_kernel, half_x, x_cells, blocks, x_ranks, x...  2.53 us
    pallas_call x1, Pallas kernels, on_device(): call(functools.partial(local_kernel, half_x, half_y, x_cells, blocks), [n...  1.87 us
    pallas_call x1, Pallas kernels, on_device(): call(functools.partial(y_inside_kernel, half_y), [near(block)], [turned,...  1.48 us
    pallas_call x1, Pallas kernels, on_device(): call(functools.partial(x_join_kernel, half_x, 'gx', x_ranks, x_rows, y_ra...  1.28 us
  transfers between devices with their start and end apart: 2, of which 2 were waited for; matrix products, arithmetic and copies ran while one was open for 0% of the time, Pallas kernels for 10%

profile of v1, /device:TPU:1, one launch (start us, length us, event | category | flops | bytes accessed | tf_op | source)
XLA Modules:
  0.0 33.3 jit_solution(14563460503965748967)
XLA Ops:
  0.0 0.0 copy-start.2
  0.0 2.5 %x_ends.1 = f32[640,128]{1,0:T(8,128)} custom-call(f32[1024,128]{1,0:T(8,128)} %bitcast.24, f32[256,128]{1,0:T(8,128)} %bitcast.27, f32[256,128]{1,0:T(8,128)} %bitcast.30), custom_call_target="tpu_custom_call" | custom-call | tf_op jit(solution)/shard_map/x_ends/pallas_call | solution.py:402
  2.5 0.0 copy-start
  2.5 0.0 copy-start.1
  2.6 8.7 %all-to-all-start = ((f32[16,40,128]{2,1,0:T(8,128)}), f32[16,40,128]{2,1,0:T(8,128)S(1)}, u32[]{:S(2)}, u32[]{:S(2)}) async-start(f32[16,40,128]{2,1,0:T(8,128)} %bitcast.9), calls=%async_computation | async-start | bytes 655360 | tf_op jit(solution)/shard_map/all_to_all | solution.py:408
  11.3 0.0 copy-done.2
  11.3 0.0 copy-done
  11.3 0.0 copy-done.1
  11.3 1.9 %local.1 = (f32[4,2,128,128]{3,2,1,0:T(8,128)S(1)}, f32[2,2,128,128]{3,2,1,0:T(8,128)S(1)}, f32[2,2,128,128]{3,2,1,0:T(8,128)S(1)}, f32[2,2,128,128]{3,2,1,0:T(8...) custom-call(f32[1024,128]{1,0:T(8,128)S(1)} %bitcast.25, f32[256,128]{1,0:T(8,128)S(1)} %bitcast.28, ...), custom_call_target="tpu_custom_call" | custom-call | tf_op jit(solution)/shard_map/local/pallas_call | solution.py:409
  13.2 6.6 %all-to-all-done = f32[16,40,128]{2,1,0:T(8,128)S(1)} async-done(((f32[16,40,128]{2,1,0:T(8,128)}), f32[16,40,128]{2,1,0:T(8,128)S(1)}, u32[]{:S(2)}, u32[]{:S(2)}) %all-to-all-start) | async-done | bytes 327712 | tf_op jit(solution)/shard_map/all_to_all | solution.py:408
  19.8 1.3 %x_join.1 = (f32[4,2,128,128]{3,2,1,0:T(8,128)S(1)}, f32[192,128]{1,0:T(8,128)}) custom-call(f32[640,128]{1,0:T(8,128)S(1)} %bitcast.26, f32[4,2,128,128]{3,2,1,0:T(8,128)S(1)} %get-tuple-element.13.inner, f32[2,2,128,128]{3,2,1,0:T(8,128)S(1)} %get-tuple-element.14.x_a, f32[2,2,128,128]{3,2,1,0:T(8,128)S(1)} %get-tuple-element.15.x_b, ...), custom_call_target="tpu_custom_call" | custom-call | tf_op jit(solution)/shard_map/x_join/pallas_call | solution.py:413
  21.1 6.2 %all-to-all-start.1 = ((f32[8,24,128]{2,1,0:T(8,128)}), f32[8,24,128]{2,1,0:T(8,128)S(1)}, u32[]{:S(2)}, u32[]{:S(2)}) async-start(f32[8,24,128]{2,1,0:T(8,128)} %bitcast.17), calls=%async_computation.1 | async-start | bytes 196608 | tf_op jit(solution)/shard_map/all_to_all | solution.py:418
  27.2 1.5 %y_inside.1.inner = f32[4,2,128,128]{3,2,1,0:T(8,128)S(1)} custom-call(f32[4,2,128,128]{3,2,1,0:T(8,128)S(1)} %get-tuple-element.20.swept, f32[256,128]{1,0:T(8,128)S(1)} %bitcast.29, f32[256,128]{1,0:T(8,128)S(1)} %bitcast.32), custom_call_target="tpu_custom_call" | custom-call | tf_op jit(solution)/shard_map/y_inside/pallas_call | solution.py:419
  28.7 3.5 %all-to-all-done.1 = f32[8,24,128]{2,1,0:T(8,128)S(1)} async-done(((f32[8,24,128]{2,1,0:T(8,128)}), f32[8,24,128]{2,1,0:T(8,128)S(1)}, u32[]{:S(2)}, u32[]{:S(2)}) %all-to-all-start.1) | async-done | bytes 98336 | tf_op jit(solution)/shard_map/all_to_all | solution.py:418
  32.2 1.0 %y_join.1 = f32[1024,128]{1,0:T(8,128)} custom-call(f32[192,128]{1,0:T(8,128)S(1)} %bitcast.33, f32[4,2,128,128]{3,2,1,0:T(8,128)S(1)} %y_inside.1.inner, f32[2,2,128,128]{3,2,1,0:T(8,128)S(1)} %get-tuple-element.16.y_a, f32[2,2,128,128]{3,2,1,0:T(8,128)S(1)} %get-tuple-element.17.y_b), custom_call_target="tpu_custom_call" | custom-call | tf_op jit(solution)/shard_map/y_join/pallas_call | solution.py:422
Async XLA Ops:
  0.0 11.3 %copy-start.2 = (f32[1,128,256]{2,1,0:T(8,128)S(1)}, f32[1,128,256]{2,1,0:T(8,128)}, u32[]{:S(2)}) copy-start(f32[1,128,256]{2,1,0:T(8,128)} %param.5) | copy-start | bytes 393220
  2.5 8.8 %copy-start = (f32[4,1,128,256]{3,2,1,0:T(8,128)S(1)}, f32[4,1,128,256]{3,2,1,0:T(8,128)}, u32[]{:S(2)}) copy-start(f32[4,1,128,256]{3,2,1,0:T(8,128)} %param.3) | copy-start | bytes 1572868
  2.5 8.8 %copy-start.1 = (f32[1,128,256]{2,1,0:T(8,128)S(1)}, f32[1,128,256]{2,1,0:T(8,128)}, u32[]{:S(2)}) copy-start(f32[1,128,256]{2,1,0:T(8,128)} %param.4) | copy-start | bytes 393220
  2.6 17.2 %all-to-all-start = ((f32[16,40,128]{2,1,0:T(8,128)}), f32[16,40,128]{2,1,0:T(8,128)S(1)}, u32[]{:S(2)}, u32[]{:S(2)}) async-start(f32[16,40,128]{2,1,0:T(8,128)} %bitcast.9), calls=%async_computation | async-start | bytes 655360 | tf_op jit(solution)/shard_map/all_to_all | solution.py:408
  21.1 11.1 %all-to-all-start.1 = ((f32[8,24,128]{2,1,0:T(8,128)}), f32[8,24,128]{2,1,0:T(8,128)S(1)}, u32[]{:S(2)}, u32[]{:S(2)}) async-start(f32[8,24,128]{2,1,0:T(8,128)} %bitcast.17), calls=%async_computation.1 | async-start | bytes 196608 | tf_op jit(solution)/shard_map/all_to_all | solution.py:418

commit v2 on v1

v2 whole, which is shorter than its diff:
```python
import functools

import jax
import jax.numpy as jnp
from jax import lax
from jax.experimental import pallas as pl
from jax.experimental.pallas import tpu as pltpu
from jax.sharding import PartitionSpec as P


FIELDS = 4
KIND = (0, 0, 0, 1)
LANES = 128
SUB = 8
COEF_ROWS = 5
QUANTITIES = 2 * COEF_ROWS + 2 * FIELDS


def recip(value):
    guess = pl.reciprocal(value, approx=True)
    return guess * (2.0 - value * guess)


def up(rows, step):
    step %= rows.shape[0]
    return pltpu.roll(rows, rows.shape[0] - step, 0) if step else rows


def down(rows, step):
    return pltpu.roll(rows, step, 0)


def row_index(rows):
    return lax.broadcasted_iota(jnp.int32, (rows, LANES), 0)


def pair(left, ground_u, link, ground_v, right):
    total_u, total_v = left + ground_u, right + ground_v
    scale = recip(total_u * total_v + link * (total_u + total_v))
    return (total_v + link) * scale, link * scale, (total_u + link) * scale


def join(link, ground_a, ground_b, face, shift):
    right, ground_v = up(link, shift), up(ground_a, shift)
    uu, uv, vv = pair(link, ground_b, face, ground_v, right)
    u_left, v_left, u_right, v_right = link * uu, link * uv, right * uv, right * vv
    joined = (
        v_left * right,
        ground_a + ground_b * u_left + ground_v * v_left,
        up(ground_b, shift) + ground_b * u_right + ground_v * v_right,
    )
    return joined, (uu, uv, vv, u_left, v_left, u_right, v_right)


def join_sources(source_a, source_b, weights, shift):
    _, _, _, u_left, v_left, u_right, v_right = weights
    source_v = up(source_a, shift)
    return (
        source_a + source_b * u_left + source_v * v_left,
        up(source_b, shift) + source_b * u_right + source_v * v_right,
    )


def schedule(count):
    nodes, rounds = list(range(count)), []
    while len(nodes) > 2:
        gone = range(1, len(nodes) - 1, 2)
        rounds.append([(nodes[i], nodes[i - 1], nodes[i + 1]) for i in gone])
        nodes = [n for i, n in enumerate(nodes) if i not in gone]
    return rounds


SHIFTS = (1, 2, 4)


def eliminate(coefs, half):
    count = len(coefs)
    ground = [1.0] * count
    link = {i: half * (coefs[i] + coefs[i + 1]) for i in range(count - 1)}
    cells, scales = {}, {}
    for round_ in schedule(count):
        for cell, low, high in round_:
            scale = recip(link[low] + link[cell] + ground[cell])
            to_low, to_high = link[low] * scale, link[cell] * scale
            ground[low] = ground[low] + to_low * ground[cell]
            ground[high] = ground[high] + to_high * ground[cell]
            link[low] = to_low * link[cell]
            cells[cell], scales[cell] = (to_low, to_high), scale
    face = half * (coefs[-1] + up(coefs[0], 1))
    chain, joins = (link[0], ground[0], ground[-1]), []
    for shift in SHIFTS:
        chain, weights = join(*chain, up(face, shift - 1), shift)
        joins.append(weights)
    return cells, scales, joins, chain


def push_sources(cells, scales, joins, sources):
    sources, scaled = list(sources), {}
    for round_ in schedule(len(sources)):
        for cell, low, high in round_:
            to_low, to_high = cells[cell]
            sources[low] = sources[low] + to_low * sources[cell]
            sources[high] = sources[high] + to_high * sources[cell]
            scaled[cell] = scales[cell] * sources[cell]
    ends, joined = (sources[0], sources[-1]), []
    for shift, weights in zip(SHIFTS, joins):
        uu, uv, vv = weights[:3]
        source_u, source_v = ends[1], up(ends[0], shift)
        joined.append((uu * source_u + uv * source_v, uv * source_u + vv * source_v))
        ends = join_sources(*ends, weights, shift)
    return scaled, joined, ends


def pull_values(cells, joins, scaled, joined, end_a, end_b):
    row = row_index(SUB)
    for shift, (u_left, v_left, u_right, v_right), (from_u, from_v) in reversed(list(zip(SHIFTS, joins, joined))):
        value_u = from_u + u_left * end_a + u_right * end_b
        value_v = from_v + v_left * end_a + v_right * end_b
        on_right = (row // shift) % 2 == 1
        end_a = jnp.where(on_right, down(value_v, shift), end_a)
        end_b = jnp.where(on_right, down(end_b, shift), value_u)
    count = len(cells) + 2
    values = {0: end_a, count - 1: end_b}
    for round_ in reversed(schedule(count)):
        for cell, low, high in round_:
            to_low, to_high = cells[cell]
            values[cell] = scaled[cell] + to_low * values[low] + to_high * values[high]
    return [values[t] for t in range(count)]


def weight_rows(count):
    return (2 * (count - 2) + 4 * len(SHIFTS)) * SUB


def source_rows(count):
    return (count - 2 + 2 * len(SHIFTS)) * SUB


def save(ref, arrays):
    for i, array in enumerate(arrays):
        ref[pl.ds(i * SUB, SUB), :] = array


def save_weights(ref, cells, joins):
    save(ref, [w for c in sorted(cells) for w in cells[c]] + [w for weights in joins for w in weights[3:]])


def save_sources(ref, scaled, joined):
    save(ref, [scaled[c] for c in sorted(scaled)] + [v for two in joined for v in two])


def load_weights(ref, count):
    def at(i):
        return ref[pl.ds(i * SUB, SUB), :]

    base = 2 * (count - 2)
    cells = {c: (at(2 * c - 2), at(2 * c - 1)) for c in range(1, count - 1)}
    return cells, [tuple(at(base + 4 * j + i) for i in range(4)) for j in range(len(SHIFTS))]


def load_sources(ref, count):
    def at(i):
        return ref[pl.ds(i * SUB, SUB), :]

    base = count - 2
    return {c: at(c - 1) for c in range(1, count - 1)}, [
        (at(base + 2 * j), at(base + 2 * j + 1)) for j in range(len(SHIFTS))
    ]


def spread(row):
    return jnp.broadcast_to(row[:1], (SUB, LANES))


def to_cells(rows):
    parts = jnp.swapaxes(rows.reshape(SUB, -1, LANES), 0, 1)
    return [parts[t] for t in range(parts.shape[0])]


def from_cells(cells):
    return jnp.swapaxes(jnp.stack(cells), 0, 1).reshape(-1, LANES)


def tiles(array):
    x_cells, y_cells = array.shape[-2:]
    split = array.reshape(-1, x_cells // SUB, SUB, y_cells // LANES, LANES)
    return split.transpose(0, 1, 3, 2, 4).reshape(-1, LANES)


def untiles(flat, shape):
    split = flat.reshape(-1, shape[-2] // SUB, shape[-1] // LANES, SUB, LANES)
    return split.transpose(0, 1, 3, 2, 4).reshape(shape)


def tile_at(field, x_tile, block, x_cells, blocks):
    return ((field * (x_cells // SUB) + x_tile) * blocks + block) * SUB


def load_x_cells(ref, field, x_cells, blocks):
    parts = to_cells(ref[pl.ds(field * x_cells * blocks, x_cells * blocks), :])
    return [
        [parts[(t // SUB * blocks + block) * SUB + t % SUB] for t in range(x_cells // SUB)] for block in range(blocks)
    ]


def load_block(ref, field, block, x_cells, blocks):
    return jnp.concatenate(
        [ref[pl.ds(tile_at(field, i, block, x_cells, blocks), SUB), :] for i in range(x_cells // SUB)]
    )


def solve_ring(quantity, ranks, rank, half):
    row = row_index(ranks)
    device = lax.rem(row + (rank + 1), ranks)
    first, last = device == 0, device == ranks - 1
    results = []
    for kind in range(2):
        first_coef, last_coef, link, ground_a, ground_b = [
            quantity(kind * COEF_ROWS + i) for i in range(COEF_ROWS)
        ]
        ground_a = ground_a + jnp.where(first, half * first_coef, 0.0)
        ground_b = ground_b + jnp.where(last, half * last_coef, 0.0)
        face = jnp.where(last, 0.0, half * (last_coef + up(first_coef, 1)))
        own = [up(x, ranks - 1) for x in (link, ground_a, ground_b)]
        left, right = up(face, ranks - 1), up(face, ranks - 2)
        fields = [f for f in range(FIELDS) if KIND[f] == kind]
        sources = [
            (quantity(2 * COEF_ROWS + 2 * f), quantity(2 * COEF_ROWS + 2 * f + 1)) for f in fields
        ]
        own_sources = [[up(x, ranks - 1) for x in pair_] for pair_ in sources]
        chain, shift = (link, ground_a, ground_b), 1
        while shift < ranks:
            joined, weights = join(*chain, up(face, shift - 1), shift)
            joined_sources = [join_sources(*s, weights, shift) for s in sources]
            if shift == 1:
                alone = row == ranks - 2
                joined = [jnp.where(alone, a, b) for a, b in zip(chain, joined)]
                joined_sources = [
                    [jnp.where(alone, a, b) for a, b in zip(old, new)]
                    for old, new in zip(sources, joined_sources)
                ]
            chain, sources, shift = joined, joined_sources, 2 * shift
        link, ground_u, ground_v = chain
        uu, uv, vv = pair(left, ground_u, link, ground_v, right)
        u_b, v_b, u_a, v_a = left * uu, left * uv, right * uv, right * vv
        link = own[0] + v_b * right
        ground_a = own[1] + ground_u * u_a + ground_v * v_a
        ground_b = own[2] + ground_u * u_b + ground_v * v_b
        scale = recip(ground_a * ground_b + link * (ground_a + ground_b))
        aa, ab, bb = (ground_b + link) * scale, link * scale, (ground_a + link) * scale
        for (source_u, source_v), (source_a, source_b) in zip(sources, own_sources):
            source_a = source_a + source_u * u_a + source_v * v_a
            source_b = source_b + source_u * u_b + source_v * v_b
            results.append((aa * source_a + ab * source_b, ab * source_a + bb * source_b))
    return results


def rotate(received, turned, ranks, rows, rank):
    for k in range(ranks):
        source = pl.multiple_of(lax.rem(rank + 1 + k, ranks) * rows, SUB)
        turned[pl.ds(k * rows, rows), :] = received[pl.ds(source, rows), :]


def coef_rows(coefs, chain):
    return (coefs[0][:1], coefs[-1][SUB - 1 :], chain[0][:1], chain[1][:1], chain[2][:1])


def x_ends_kernel(
    half, x_cells, blocks, ranks, rows,
    fields, viscosity, diffusivity, message, weights, pushed,
    line, fields_here, viscosity_here, diffusivity_here, arrived,
):
    per_field = x_cells * blocks
    copies = [
        pltpu.make_async_copy(viscosity, viscosity_here, arrived.at[0]),
        pltpu.make_async_copy(diffusivity, diffusivity_here, arrived.at[1]),
    ]
    for f in range(FIELDS):
        part = pl.ds(f * per_field, per_field)
        copies.append(pltpu.make_async_copy(fields.at[part], fields_here.at[part], arrived.at[2 + f]))
    for copy in copies:
        copy.start()
    line[...] = jnp.zeros_like(line)

    def put(quantity, block, value):
        at = quantity * blocks + block
        line[at : at + 1, :] = value

    plans = {}
    for copy in copies[:2]:
        copy.wait()
    for kind, coef in enumerate((viscosity_here, diffusivity_here)):
        for block, coefs in enumerate(load_x_cells(coef, 0, x_cells, blocks)):
            *plan, chain = eliminate(coefs, half)
            plans[kind, block] = plan
            save_weights(weights.at[kind, block], plan[0], plan[2])
            for i, value in enumerate(coef_rows(coefs, chain)):
                put(kind * COEF_ROWS + i, block, value)
    for copy in copies[2:]:
        copy.wait()
    for f in range(FIELDS):
        for block, sources in enumerate(load_x_cells(fields_here, f, x_cells, blocks)):
            scaled, joined, ends = push_sources(*plans[KIND[f], block], sources)
            save_sources(pushed.at[f, block], scaled, joined)
            put(2 * COEF_ROWS + 2 * f, block, ends[0][:1])
            put(2 * COEF_ROWS + 2 * f + 1, block, ends[1][:1])
    for k in range(ranks):
        message[pl.ds(k * rows, rows), :] = line[...]


def x_join_kernel(
    half_x, half_y, x_cells, blocks, axis, ranks, rows, y_ranks, y_rows,
    received, x_weights, x_pushed, viscosity, diffusivity, message, weights, pushed,
    turned, line,
):
    rank = lax.axis_index(axis)
    count, y_count = x_cells // SUB, blocks * LANES // SUB
    rotate(received, turned, ranks, rows, rank)
    line[...] = jnp.zeros_like(line)
    plans = []
    for kind, coef in enumerate((viscosity, diffusivity)):
        coefs = to_cells(jnp.concatenate([load_block(coef, 0, b, x_cells, blocks).T for b in range(blocks)]))
        *plan, chain = eliminate(coefs, half_y)
        plans.append(plan)
        save_weights(weights.at[kind], plan[0], plan[2])
        for i, value in enumerate(coef_rows(coefs, chain)):
            line[kind * COEF_ROWS + i : kind * COEF_ROWS + i + 1, :] = value
    lines = [[] for _ in range(FIELDS)]
    for block in range(blocks):
        ends = solve_ring(
            lambda q: turned[pl.ds(q * blocks + block, ranks, stride=rows), :], ranks, rank, half_x
        )
        for f in range(FIELDS):
            end_a, end_b = [spread(e) for e in ends[f]]
            values = pull_values(
                *load_weights(x_weights.at[KIND[f], block], count), *load_sources(x_pushed.at[f, block], count), end_a, end_b
            )
            lines[f].append(from_cells(values).T)
    for f in range(FIELDS):
        scaled, joined, ends = push_sources(*plans[KIND[f]], to_cells(jnp.concatenate(lines[f])))
        save_sources(pushed.at[f], scaled, joined)
        at = 2 * COEF_ROWS + 2 * f
        line[at : at + 1, :] = ends[0][:1]
        line[at + 1 : at + 2, :] = ends[1][:1]
    for k in range(y_ranks):
        message[pl.ds(k * y_rows, y_rows), :] = line[...]


def y_join_kernel(
    half, x_cells, blocks, axis, ranks, rows,
    received, weights, pushed, updated, turned, here, left,
):
    per_field = x_cells * blocks
    count = blocks * LANES // SUB
    rank = lax.axis_index(axis)
    rotate(received, turned, ranks, rows, rank)
    ends = solve_ring(lambda q: turned[pl.ds(q, ranks, stride=rows), :], ranks, rank, half)
    copies = []
    for f in range(FIELDS):
        end_a, end_b = [spread(e) for e in ends[f]]
        values = pull_values(
            *load_weights(weights.at[KIND[f]], count), *load_sources(pushed.at[f], count), end_a, end_b
        )
        lines = from_cells(values)
        for block in range(blocks):
            value = lines[block * LANES : (block + 1) * LANES].T
            for i in range(x_cells // SUB):
                here[pl.ds(tile_at(f, i, block, x_cells, blocks), SUB), :] = value[i * SUB : (i + 1) * SUB]
        part = pl.ds(f * per_field, per_field)
        copies.append(pltpu.make_async_copy(here.at[part], updated.at[part], left.at[f]))
        copies[-1].start()
    for copy in copies:
        copy.wait()


def call(kernel, outs, scratch, name, **kw):
    return pl.pallas_call(
        kernel,
        out_shape=outs,
        scratch_shapes=[pltpu.VMEM(s, jnp.float32) if isinstance(s, tuple) else s for s in scratch],
        compiler_params=pltpu.CompilerParams(vmem_limit_bytes=24 * 1024 * 1024),
        name=name,
        **kw,
    )


def near(shape):
    return pltpu.VMEM(shape, jnp.float32)


def far(shape):
    return pltpu.HBM(shape, jnp.float32)


def padded(rows):
    return -(-rows // SUB) * SUB


def on_device(x_ranks, y_ranks, fields, viscosity, diffusivity):
    _, _, x_cells, y_cells = fields.shape
    blocks = y_cells // LANES
    half_x, half_y = 0.5 * float(x_cells * x_cells), 0.5 * float(y_cells * y_cells)
    x_rows, y_rows = padded(QUANTITIES * blocks), padded(QUANTITIES)
    x_count, y_count = x_cells // SUB, y_cells // SUB
    args = [tiles(a) for a in (fields, viscosity, diffusivity)]
    sizes = [a.shape for a in args]
    in_hbm = [pltpu.with_memory_space_constraint(a, pltpu.HBM) for a in args]

    message, x_weights, x_pushed = call(
        functools.partial(x_ends_kernel, half_x, x_cells, blocks, x_ranks, x_rows),
        [
            near((x_ranks * x_rows, LANES)),
            near((2, blocks, weight_rows(x_count), LANES)),
            near((FIELDS, blocks, source_rows(x_count), LANES)),
        ],
        [(x_rows, LANES), *sizes, pltpu.SemaphoreType.DMA((2 + FIELDS,))], "x_ends",
        in_specs=[pl.BlockSpec(memory_space=pltpu.HBM)] * 3,
    )(*in_hbm)
    received = lax.all_to_all(message.reshape(x_ranks, x_rows, LANES), "gx", 0, 0, tiled=True)
    message, y_weights, y_pushed = call(
        functools.partial(x_join_kernel, half_x, half_y, x_cells, blocks, "gx", x_ranks, x_rows, y_ranks, y_rows),
        [
            near((y_ranks * y_rows, LANES)),
            near((2, weight_rows(y_count), LANES)),
            near((FIELDS, source_rows(y_count), LANES)),
        ],
        [(x_ranks * x_rows, LANES), (y_rows, LANES)],
        "x_join",
    )(received.reshape(x_ranks * x_rows, LANES), x_weights, x_pushed, *args[1:])
    received = lax.all_to_all(message.reshape(y_ranks, y_rows, LANES), "gy", 0, 0, tiled=True)
    (updated,) = call(
        functools.partial(y_join_kernel, half_y, x_cells, blocks, "gy", y_ranks, y_rows),
        [far(sizes[0])],
        [(y_ranks * y_rows, LANES), sizes[0], pltpu.SemaphoreType.DMA((FIELDS,))], "y_join",
        out_specs=[pl.BlockSpec(memory_space=pltpu.HBM)],
    )(received.reshape(y_ranks * y_rows, LANES), y_weights, y_pushed)
    return untiles(updated, fields.shape)


def solution(mesh):
    placed = (P(None, None, "gx", "gy"), P(None, "gx", "gy"), P(None, "gx", "gy"))
    return jax.shard_map(
        functools.partial(on_device, mesh.shape["gx"], mesh.shape["gy"]),
        mesh=mesh, in_specs=placed, out_specs=P(None, None, "gx", "gy"), check_vma=False,
    )
```

time: 33.6 us -> 32 us (0.952)
  blocking collectives: 0 us -> 27.9 us
  starting transfers between devices: 14.9 us -> 0 us
  waiting for transfers between devices: 10.1 us -> 0 us
  Pallas kernels: 8.21 us -> 3.76 us
    all_to_all x0 -> x2, blocking collectives: none -> 27.9 us  [the longest x1 17 us: on_device(): lax.all_to_all(message.reshape(x_ranks, x_rows, LANES), 'gx', 0, 0, tiled...]
    all_to_all x2 -> x0, starting transfers between devices: 14.9 us -> none  [the longest x1 8.74 us: on_device(): lax.all_to_all(message.reshape(x_ranks, x_rows, LANES), 'gx', 0, 0, tiled...]
    all_to_all x2 -> x0, waiting for transfers between devices: 10.1 us -> none  [the longest x1 6.57 us: on_device(): lax.all_to_all(message.reshape(x_ranks, x_rows, LANES), 'gx', 0, 0, tiled...]
    pallas_call x4 -> x2, Pallas kernels: 5.68 us -> 2.21 us  [the longest x1 1.16 us: on_device(): call(functools.partial(y_join_kernel, half_y, x_cells, blocks, 'gy', y_ra...]
    pallas_call x1, Pallas kernels: 2.53 us -> 1.55 us  [on_device(): call(functools.partial(x_ends_kernel, half_x, x_cells, blocks, x_ranks, x...]
  transfers between devices with their start and end apart: 2 -> 0, of which waited for: 2 -> 0; matrix products, arithmetic and copies ran while one was open for 0% -> 0% of each run, Pallas kernels for 10% -> 0%
where the time goes in v2:
time: 32 us; the launch traced here: 31.8 us
  blocking collectives  27.9 us (87%)
  Pallas kernels  3.76 us (12%)
    all_to_all x1, blocking collectives, on_device(): lax.all_to_all(message.reshape(x_ranks, x_rows, LANES), 'gx', 0, 0, tiled...  17 us
    all_to_all x1, blocking collectives, on_device(): lax.all_to_all(message.reshape(y_ranks, y_rows, LANES), 'gy', 0, 0, tiled...  10.9 us
    pallas_call x1, Pallas kernels, on_device(): call(functools.partial(x_ends_kernel, half_x, x_cells, blocks, x_ranks, x...  1.55 us
    pallas_call x1, Pallas kernels, on_device(): call(functools.partial(y_join_kernel, half_y, x_cells, blocks, 'gy', y_ra...  1.16 us
    pallas_call x1, Pallas kernels, on_device(): call(functools.partial(x_join_kernel, half_x, half_y, x_cells, blocks, 'g...  1.05 us

profile of v2, /device:TPU:1, one launch (start us, length us, event | category | flops | bytes accessed | tf_op | source)
XLA Modules:
  0.0 31.8 jit_solution(9955788069208278579)
XLA Ops:
  0.0 1.6 %x_ends.1 = (f32[640,128]{1,0:T(8,128)S(1)}, f32[2,2,320,128]{3,2,1,0:T(8,128)S(1)}, f32[4,2,160,128]{3,2,1,0:T(8,128)S(1)}) custom-call(f32[1024,128]{1,0:T(8,128)} %bitcast.32, f32[256,128]{1,0:T(8,128)} %bitcast.25, f32[256,128]{1,0:T(8,128)} %bitcast.27), custom_call_target="tpu_custom_call" | custom-call | tf_op jit(solution)/shard_map/x_ends/pallas_call | solution.py:409
  1.6 0.0 copy-start
  1.6 0.0 copy-start.1
  1.6 17.0 %all_to_all.10 = f32[16,40,128]{2,1,0:T(8,128)S(1)} all-to-all(f32[16,40,128]{2,1,0:T(8,128)S(1)} %bitcast.30), channel_id=1, replica_groups=mesh['gx'=16,'gy'=8] {'gx'}, dimensions={0} | all-to-all | bytes 655360 | tf_op jit(solution)/shard_map/all_to_all | solution.py:419
  18.6 0.0 copy-done
  18.6 0.0 copy-done.1
  18.6 1.1 %x_join.1 = (f32[192,128]{1,0:T(8,128)S(1)}, f32[2,576,128]{2,1,0:T(8,128)S(1)}, f32[4,288,128]{2,1,0:T(8,128)S(1)}) custom-call(f32[640,128]{1,0:T(8,128)S(1)} %bitcast.24, f32[2,2,320,128]{3,2,1,0:T(8,128)S(1)} %get-tuple-element.12.x_weights, f32[4,2,160,128]{3,2,1,0:T(8,128)S(1)} %get-tuple-element.13.x_pushed, f32[256,128]{1,0:T(8,128)S(1)} %bitcast.26, ...), custom_call_target="tpu_custom_call" | custom-call | tf_op jit(solution)/shard_map/x_join/pallas_call | solution.py:420
  19.7 10.9 %all_to_all.11 = f32[8,24,128]{2,1,0:T(8,128)S(1)} all-to-all(f32[8,24,128]{2,1,0:T(8,128)S(1)} %bitcast.31), channel_id=1, replica_groups=mesh['gx'=16,'gy'=8] {'gy'}, dimensions={0} | all-to-all | bytes 196608 | tf_op jit(solution)/shard_map/all_to_all | solution.py:430
  30.6 1.2 %y_join.1 = f32[1024,128]{1,0:T(8,128)} custom-call(f32[192,128]{1,0:T(8,128)S(1)} %bitcast.29, f32[2,576,128]{2,1,0:T(8,128)S(1)} %get-tuple-element.15.weights, f32[4,288,128]{2,1,0:T(8,128)S(1)} %get-tuple-element.16.pushed), custom_call_target="tpu_custom_call" | custom-call | tf_op jit(solution)/shard_map/y_join/pallas_call | solution.py:431
Async XLA Ops:
  1.6 17.0 %copy-start = (f32[1,128,256]{2,1,0:T(8,128)S(1)}, f32[1,128,256]{2,1,0:T(8,128)}, u32[]{:S(2)}) copy-start(f32[1,128,256]{2,1,0:T(8,128)} %param.4) | copy-start | bytes 393220
  1.6 17.0 %copy-start.1 = (f32[1,128,256]{2,1,0:T(8,128)S(1)}, f32[1,128,256]{2,1,0:T(8,128)}, u32[]{:S(2)}) copy-start(f32[1,128,256]{2,1,0:T(8,128)} %param.5) | copy-start | bytes 393220

commit v3 on v2

--- a/solution.py
+++ b/solution.py
@@ -40,25 +40,38 @@
     return (total_v + link) * scale, link * scale, (total_u + link) * scale
 
 
-def join(link, ground_a, ground_b, face, shift):
-    right, ground_v = up(link, shift), up(ground_a, shift)
-    uu, uv, vv = pair(link, ground_b, face, ground_v, right)
+def join_two(low, face, high):
+    link, ground_a, ground_u = low
+    right, ground_v, ground_b = high
+    uu, uv, vv = pair(link, ground_u, face, ground_v, right)
     u_left, v_left, u_right, v_right = link * uu, link * uv, right * uv, right * vv
     joined = (
         v_left * right,
-        ground_a + ground_b * u_left + ground_v * v_left,
-        up(ground_b, shift) + ground_b * u_right + ground_v * v_right,
+        ground_a + ground_u * u_left + ground_v * v_left,
+        ground_b + ground_u * u_right + ground_v * v_right,
     )
     return joined, (uu, uv, vv, u_left, v_left, u_right, v_right)
 
 
-def join_sources(source_a, source_b, weights, shift):
+def join_two_sources(low, weights, high):
     _, _, _, u_left, v_left, u_right, v_right = weights
-    source_v = up(source_a, shift)
+    (source_a, source_u), (source_v, source_b) = low, high
     return (
-        source_a + source_b * u_left + source_v * v_left,
-        up(source_b, shift) + source_b * u_right + source_v * v_right,
+        source_a + source_u * u_left + source_v * v_left,
+        source_b + source_u * u_right + source_v * v_right,
     )
+
+
+def shifted(arrays, shift):
+    return [up(x, shift) for x in arrays]
+
+
+def join(chain, face, shift):
+    return join_two(chain, face, shifted(chain, shift))
+
+
+def join_sources(ends, weights, shift):
+    return join_two_sources(ends, weights, shifted(ends, shift))
 
 
 def schedule(count):
@@ -89,7 +102,7 @@
     face = half * (coefs[-1] + up(coefs[0], 1))
     chain, joins = (link[0], ground[0], ground[-1]), []
     for shift in SHIFTS:
-        chain, weights = join(*chain, up(face, shift - 1), shift)
+        chain, weights = join(chain, up(face, shift - 1), shift)
         joins.append(weights)
     return cells, scales, joins, chain
 
@@ -107,7 +120,7 @@
         uu, uv, vv = weights[:3]
         source_u, source_v = ends[1], up(ends[0], shift)
         joined.append((uu * source_u + uv * source_v, uv * source_u + vv * source_v))
-        ends = join_sources(*ends, weights, shift)
+        ends = join_sources(ends, weights, shift)
     return scaled, joined, ends
 
 
@@ -210,36 +223,51 @@
 
 
 def solve_ring(quantity, ranks, rank, half):
-    row = row_index(ranks)
-    device = lax.rem(row + (rank + 1), ranks)
-    first, last = device == 0, device == ranks - 1
+    step = max(1, ranks // SUB)
+    count = ranks // step
+    device = [lax.rem(row_index(count) * step + (rank + 1 + k), ranks) for k in range(step)]
+    last_row = row_index(count) == count - 1
     results = []
     for kind in range(2):
-        first_coef, last_coef, link, ground_a, ground_b = [
-            quantity(kind * COEF_ROWS + i) for i in range(COEF_ROWS)
+        chains, sources, first_coefs, last_coefs = [], [], [], []
+        fields = [f for f in range(FIELDS) if KIND[f] == kind]
+        for k in range(step):
+            first, last, link, ground_a, ground_b = [
+                quantity(kind * COEF_ROWS + i, k, step) for i in range(COEF_ROWS)
+            ]
+            ground_a = ground_a + jnp.where(device[k] == 0, half * first, 0.0)
+            ground_b = ground_b + jnp.where(device[k] == ranks - 1, half * last, 0.0)
+            chains.append((link, ground_a, ground_b))
+            first_coefs.append(first)
+            last_coefs.append(last)
+            sources.append([[quantity(2 * COEF_ROWS + 2 * f + end, k, step) for end in range(2)] for f in fields])
+        first_coefs.append(up(first_coefs[0], 1))
+        faces = [
+            jnp.where(device[k] == ranks - 1, 0.0, half * (last_coefs[k] + first_coefs[k + 1])) for k in range(step)
         ]
-        ground_a = ground_a + jnp.where(first, half * first_coef, 0.0)
-        ground_b = ground_b + jnp.where(last, half * last_coef, 0.0)
-        face = jnp.where(last, 0.0, half * (last_coef + up(first_coef, 1)))
-        own = [up(x, ranks - 1) for x in (link, ground_a, ground_b)]
-        left, right = up(face, ranks - 1), up(face, ranks - 2)
-        fields = [f for f in range(FIELDS) if KIND[f] == kind]
-        sources = [
-            (quantity(2 * COEF_ROWS + 2 * f), quantity(2 * COEF_ROWS + 2 * f + 1)) for f in fields
-        ]
-        own_sources = [[up(x, ranks - 1) for x in pair_] for pair_ in sources]
-        chain, shift = (link, ground_a, ground_b), 1
-        while shift < ranks:
-            joined, weights = join(*chain, up(face, shift - 1), shift)
-            joined_sources = [join_sources(*s, weights, shift) for s in sources]
-            if shift == 1:
-                alone = row == ranks - 2
+        own = shifted(chains[-1], count - 1)
+        own_sources = [shifted(s, count - 1) for s in sources[-1]]
+        left = up(faces[-1], count - 1)
+        right = up(faces[step - 2], count - 1) if step > 1 else up(faces[0], count - 2)
+
+        if step == 1:
+            (chain,), (ends,), shift = chains, sources, 1
+        else:
+            joined, weights = join_two(chains[0], faces[0], chains[1])
+            chain = [jnp.where(last_row, a, b) for a, b in zip(chains[0], joined)]
+            ends = [
+                [jnp.where(last_row, a, b) for a, b in zip(low, join_two_sources(low, weights, high))]
+                for low, high in zip(*sources)
+            ]
+            shift = 1
+        while shift < count:
+            joined, weights = join(chain, up(faces[-1], shift - 1), shift)
+            joined_ends = [join_sources(s, weights, shift) for s in ends]
+            if shift == 1 and step == 1:
+                alone = row_index(count) == count - 2
                 joined = [jnp.where(alone, a, b) for a, b in zip(chain, joined)]
-                joined_sources = [
-                    [jnp.where(alone, a, b) for a, b in zip(old, new)]
-                    for old, new in zip(sources, joined_sources)
-                ]
-            chain, sources, shift = joined, joined_sources, 2 * shift
+                joined_ends = [[jnp.where(alone, a, b) for a, b in zip(*two)] for two in zip(ends, joined_ends)]
+            chain, ends, shift = joined, joined_ends, 2 * shift
         link, ground_u, ground_v = chain
         uu, uv, vv = pair(left, ground_u, link, ground_v, right)
         u_b, v_b, u_a, v_a = left * uu, left * uv, right * uv, right * vv
@@ -248,17 +276,29 @@
         ground_b = own[2] + ground_u * u_b + ground_v * v_b
         scale = recip(ground_a * ground_b + link * (ground_a + ground_b))
         aa, ab, bb = (ground_b + link) * scale, link * scale, (ground_a + link) * scale
-        for (source_u, source_v), (source_a, source_b) in zip(sources, own_sources):
+        for (source_u, source_v), (source_a, source_b) in zip(ends, own_sources):
             source_a = source_a + source_u * u_a + source_v * v_a
             source_b = source_b + source_u * u_b + source_v * v_b
             results.append((aa * source_a + ab * source_b, ab * source_a + bb * source_b))
     return results
 
 
+def received_rows(turned, ranks, rows, blocks, block):
+    def quantity(q, k, step):
+        at = k * spaced(rows) + q * blocks + block
+        return turned[pl.ds(at, ranks // step, stride=step * spaced(rows)), :]
+
+    return quantity
+
+
+def spaced(rows):
+    return rows | 1
+
+
 def rotate(received, turned, ranks, rows, rank):
     for k in range(ranks):
-        source = pl.multiple_of(lax.rem(rank + 1 + k, ranks) * rows, SUB)
-        turned[pl.ds(k * rows, rows), :] = received[pl.ds(source, rows), :]
+        source = lax.rem(rank + 1 + k, ranks) * rows
+        turned[pl.ds(k * spaced(rows), rows), :] = received[pl.ds(source, rows), :]
 
 
 def coef_rows(coefs, chain):
@@ -280,7 +320,6 @@
         copies.append(pltpu.make_async_copy(fields.at[part], fields_here.at[part], arrived.at[2 + f]))
     for copy in copies:
         copy.start()
-    line[...] = jnp.zeros_like(line)
 
     def put(quantity, block, value):
         at = quantity * blocks + block
@@ -316,7 +355,6 @@
     rank = lax.axis_index(axis)
     count, y_count = x_cells // SUB, blocks * LANES // SUB
     rotate(received, turned, ranks, rows, rank)
-    line[...] = jnp.zeros_like(line)
     plans = []
     for kind, coef in enumerate((viscosity, diffusivity)):
         coefs = to_cells(jnp.concatenate([load_block(coef, 0, b, x_cells, blocks).T for b in range(blocks)]))
@@ -327,9 +365,7 @@
             line[kind * COEF_ROWS + i : kind * COEF_ROWS + i + 1, :] = value
     lines = [[] for _ in range(FIELDS)]
     for block in range(blocks):
-        ends = solve_ring(
-            lambda q: turned[pl.ds(q * blocks + block, ranks, stride=rows), :], ranks, rank, half_x
-        )
+        ends = solve_ring(received_rows(turned, ranks, rows, blocks, block), ranks, rank, half_x)
         for f in range(FIELDS):
             end_a, end_b = [spread(e) for e in ends[f]]
             values = pull_values(
@@ -354,7 +390,7 @@
     count = blocks * LANES // SUB
     rank = lax.axis_index(axis)
     rotate(received, turned, ranks, rows, rank)
-    ends = solve_ring(lambda q: turned[pl.ds(q, ranks, stride=rows), :], ranks, rank, half)
+    ends = solve_ring(received_rows(turned, ranks, rows, 1, 0), ranks, rank, half)
     copies = []
     for f in range(FIELDS):
         end_a, end_b = [spread(e) for e in ends[f]]
@@ -392,15 +428,16 @@
     return pltpu.HBM(shape, jnp.float32)
 
 
-def padded(rows):
-    return -(-rows // SUB) * SUB
+def exchange(message, ranks, axis):
+    flat = message.reshape(ranks, 1, -1)
+    return lax.all_to_all(flat, axis, 0, 0, tiled=True).reshape(-1, LANES)
 
 
 def on_device(x_ranks, y_ranks, fields, viscosity, diffusivity):
     _, _, x_cells, y_cells = fields.shape
     blocks = y_cells // LANES
     half_x, half_y = 0.5 * float(x_cells * x_cells), 0.5 * float(y_cells * y_cells)
-    x_rows, y_rows = padded(QUANTITIES * blocks), padded(QUANTITIES)
+    x_rows, y_rows = QUANTITIES * blocks, QUANTITIES
     x_count, y_count = x_cells // SUB, y_cells // SUB
     args = [tiles(a) for a in (fields, viscosity, diffusivity)]
     sizes = [a.shape for a in args]
@@ -416,7 +453,7 @@
         [(x_rows, LANES), *sizes, pltpu.SemaphoreType.DMA((2 + FIELDS,))], "x_ends",
         in_specs=[pl.BlockSpec(memory_space=pltpu.HBM)] * 3,
     )(*in_hbm)
-    received = lax.all_to_all(message.reshape(x_ranks, x_rows, LANES), "gx", 0, 0, tiled=True)
+    received = exchange(message, x_ranks, "gx")
     message, y_weights, y_pushed = call(
         functools.partial(x_join_kernel, half_x, half_y, x_cells, blocks, "gx", x_ranks, x_rows, y_ranks, y_rows),
         [
@@ -424,16 +461,16 @@
             near((2, weight_rows(y_count), LANES)),
             near((FIELDS, source_rows(y_count), LANES)),
         ],
-        [(x_ranks * x_rows, LANES), (y_rows, LANES)],
+        [(x_ranks * spaced(x_rows), LANES), (y_rows, LANES)],
         "x_join",
-    )(received.reshape(x_ranks * x_rows, LANES), x_weights, x_pushed, *args[1:])
-    received = lax.all_to_all(message.reshape(y_ranks, y_rows, LANES), "gy", 0, 0, tiled=True)
+    )(received, x_weights, x_pushed, *args[1:])
+    received = exchange(message, y_ranks, "gy")
     (updated,) = call(
         functools.partial(y_join_kernel, half_y, x_cells, blocks, "gy", y_ranks, y_rows),
         [far(sizes[0])],
-        [(y_ranks * y_rows, LANES), sizes[0], pltpu.SemaphoreType.DMA((FIELDS,))], "y_join",
+        [(y_ranks * spaced(y_rows), LANES), sizes[0], pltpu.SemaphoreType.DMA((FIELDS,))], "y_join",
         out_specs=[pl.BlockSpec(memory_space=pltpu.HBM)],
-    )(received.reshape(y_ranks * y_rows, LANES), y_weights, y_pushed)
+    )(received, y_weights, y_pushed)
     return untiles(updated, fields.shape)
 
 

time: 32 us -> 31.4 us (0.981)
  blocking collectives: 27.9 us -> 27.5 us
    all_to_all x2, blocking collectives: 27.9 us -> 27.5 us  [exchange(): return lax.all_to_all(flat, axis, 0, 0, tiled=True).reshape(-1, LANES)]
where the time goes in v3:
time: 31.4 us; the launch traced here: 31.2 us
  blocking collectives  27.5 us (88%)
  Pallas kernels  3.63 us (12%)
    all_to_all x2, blocking collectives, exchange(): return lax.all_to_all(flat, axis, 0, 0, tiled=True).reshape(-1, LANES)  27.5 us
    pallas_call x1, Pallas kernels, on_device(): call(functools.partial(x_ends_kernel, half_x, x_cells, blocks, x_ranks, x...  1.55 us
    pallas_call x1, Pallas kernels, on_device(): call(functools.partial(y_join_kernel, half_y, x_cells, blocks, 'gy', y_ra...  1.14 us
    pallas_call x1, Pallas kernels, on_device(): call(functools.partial(x_join_kernel, half_x, half_y, x_cells, blocks, 'g...  0.94 us

profile of v3, /device:TPU:1, one launch (start us, length us, event | category | flops | bytes accessed | tf_op | source)
XLA Modules:
  0.0 31.2 jit_solution(14329754074887676050)
XLA Ops:
  0.0 1.6 %x_ends.1 = (f32[576,128]{1,0:T(8,128)S(1)}, f32[2,2,320,128]{3,2,1,0:T(8,128)S(1)}, f32[4,2,160,128]{3,2,1,0:T(8,128)S(1)}) custom-call(f32[1024,128]{1,0:T(8,128)} %bitcast.32, f32[256,128]{1,0:T(8,128)} %bitcast.25, f32[256,128]{1,0:T(8,128)} %bitcast.27), custom_call_target="tpu_custom_call" | custom-call | tf_op jit(solution)/shard_map/x_ends/pallas_call | solution.py:446
  1.6 0.0 copy-start
  1.6 0.0 copy-start.1
  1.6 16.7 %all_to_all.10 = f32[16,1,4608]{2,1,0:T(1,128)S(1)} all-to-all(f32[16,1,4608]{2,1,0:T(1,128)S(1)} %bitcast.30), channel_id=1, replica_groups=mesh['gx'=16,'gy'=8] {'gx'}, dimensions={0} | all-to-all | bytes 589824 | tf_op jit(solution)/shard_map/all_to_all | solution.py:433
  18.2 0.0 copy-done
  18.2 0.0 copy-done.1
  18.2 0.9 %x_join.1 = (f32[144,128]{1,0:T(8,128)S(1)}, f32[2,576,128]{2,1,0:T(8,128)S(1)}, f32[4,288,128]{2,1,0:T(8,128)S(1)}) custom-call(f32[576,128]{1,0:T(8,128)S(1)} %bitcast.24, f32[2,2,320,128]{3,2,1,0:T(8,128)S(1)} %get-tuple-element.12.x_weights, f32[4,2,160,128]{3,2,1,0:T(8,128)S(1)} %get-tuple-element.13.x_pushed, f32[256,128]{1,0:T(8,128)S(1)} %bitcast.26, ...), custom_call_target="tpu_custom_call" | custom-call | tf_op jit(solution)/shard_map/x_join/pallas_call | solution.py:457
  19.2 10.8 %all_to_all.11 = f32[8,1,2304]{2,1,0:T(1,128)S(1)} all-to-all(f32[8,1,2304]{2,1,0:T(1,128)S(1)} %bitcast.31), channel_id=1, replica_groups=mesh['gx'=16,'gy'=8] {'gy'}, dimensions={0} | all-to-all | bytes 147456 | tf_op jit(solution)/shard_map/all_to_all | solution.py:433
  30.0 1.1 %y_join.1 = f32[1024,128]{1,0:T(8,128)} custom-call(f32[144,128]{1,0:T(8,128)S(1)} %bitcast.29, f32[2,576,128]{2,1,0:T(8,128)S(1)} %get-tuple-element.15.weights, f32[4,288,128]{2,1,0:T(8,128)S(1)} %get-tuple-element.16.pushed), custom_call_target="tpu_custom_call" | custom-call | tf_op jit(solution)/shard_map/y_join/pallas_call | solution.py:468
Async XLA Ops:
  1.6 16.7 %copy-start = (f32[1,128,256]{2,1,0:T(8,128)S(1)}, f32[1,128,256]{2,1,0:T(8,128)}, u32[]{:S(2)}) copy-start(f32[1,128,256]{2,1,0:T(8,128)} %param.4) | copy-start | bytes 393220
  1.6 16.7 %copy-start.1 = (f32[1,128,256]{2,1,0:T(8,128)S(1)}, f32[1,128,256]{2,1,0:T(8,128)}, u32[]{:S(2)}) copy-start(f32[1,128,256]{2,1,0:T(8,128)} %param.5) | copy-start | bytes 393220

commit v4 on v3

--- a/solution.py
+++ b/solution.py
@@ -301,6 +301,14 @@
         turned[pl.ds(k * spaced(rows), rows), :] = received[pl.ds(source, rows), :]
 
 
+def place(parts, turned, ranks, rows, rank):
+    for k, other, message in parts:
+        chip = lax.bitwise_xor(lax.div(rank, 2), k)
+        device = 2 * chip + lax.bitwise_xor(lax.rem(rank, 2), int(other))
+        at = lax.rem(device + ranks - rank - 1, ranks) * spaced(rows)
+        turned[pl.ds(at, rows), :] = message
+
+
 def coef_rows(coefs, chain):
     return (coefs[0][:1], coefs[-1][SUB - 1 :], chain[0][:1], chain[1][:1], chain[2][:1])
 
@@ -348,9 +356,9 @@
 
 
 def x_join_kernel(
-    half_x, half_y, x_cells, blocks, axis, ranks, rows, y_ranks, y_rows,
+    half_x, half_y, x_cells, blocks, axis, ranks, rows,
     received, x_weights, x_pushed, viscosity, diffusivity, message, weights, pushed,
-    turned, line,
+    turned,
 ):
     rank = lax.axis_index(axis)
     count, y_count = x_cells // SUB, blocks * LANES // SUB
@@ -362,7 +370,7 @@
         plans.append(plan)
         save_weights(weights.at[kind], plan[0], plan[2])
         for i, value in enumerate(coef_rows(coefs, chain)):
-            line[kind * COEF_ROWS + i : kind * COEF_ROWS + i + 1, :] = value
+            message[kind * COEF_ROWS + i : kind * COEF_ROWS + i + 1, :] = value
     lines = [[] for _ in range(FIELDS)]
     for block in range(blocks):
         ends = solve_ring(received_rows(turned, ranks, rows, blocks, block), ranks, rank, half_x)
@@ -376,20 +384,23 @@
         scaled, joined, ends = push_sources(*plans[KIND[f]], to_cells(jnp.concatenate(lines[f])))
         save_sources(pushed.at[f], scaled, joined)
         at = 2 * COEF_ROWS + 2 * f
-        line[at : at + 1, :] = ends[0][:1]
-        line[at + 1 : at + 2, :] = ends[1][:1]
-    for k in range(y_ranks):
-        message[pl.ds(k * y_rows, y_rows), :] = line[...]
+        message[at : at + 1, :] = ends[0][:1]
+        message[at + 1 : at + 2, :] = ends[1][:1]
 
 
 def y_join_kernel(
-    half, x_cells, blocks, axis, ranks, rows,
-    received, weights, pushed, updated, turned, here, left,
+    half, x_cells, blocks, axis, ranks, rows, layout,
+    *refs,
 ):
+    *chips, weights, pushed, updated, turned, here, left = refs
     per_field = x_cells * blocks
     count = blocks * LANES // SUB
     rank = lax.axis_index(axis)
-    rotate(received, turned, ranks, rows, rank)
+    parts = []
+    for (k, others), ref in zip(layout, chips):
+        for i, other in enumerate(others):
+            parts.append((k, other, ref[pl.ds(i * rows, rows), :]))
+    place(parts, turned, ranks, rows, rank)
     ends = solve_ring(received_rows(turned, ranks, rows, 1, 0), ranks, rank, half)
     copies = []
     for f in range(FIELDS):
@@ -433,6 +444,25 @@
     return lax.all_to_all(flat, axis, 0, 0, tiled=True).reshape(-1, LANES)
 
 
+def exchange_chips(message, ranks, axis):
+    def send(array, step):
+        return lax.ppermute(array, axis, [(i, i ^ step) for i in range(ranks)])
+
+    chips = range(1, ranks // 2)
+    early = chips[2 - 1]
+    near_chip = send(message, 2 * early)
+    other = send(message, 1)
+    both = jnp.concatenate([message, other])
+    layout, arrays = [(0, (False, True))], [both]
+    for k in chips:
+        if k != early:
+            layout.append((k, (False, True)))
+            arrays.append(send(both, 2 * k))
+    layout += [(early, (False,)), (early, (True,))]
+    arrays += [near_chip, send(near_chip, 1)]
+    return layout, arrays
+
+
 def on_device(x_ranks, y_ranks, fields, viscosity, diffusivity):
     _, _, x_cells, y_cells = fields.shape
     blocks = y_cells // LANES
@@ -455,22 +485,22 @@
     )(*in_hbm)
     received = exchange(message, x_ranks, "gx")
     message, y_weights, y_pushed = call(
-        functools.partial(x_join_kernel, half_x, half_y, x_cells, blocks, "gx", x_ranks, x_rows, y_ranks, y_rows),
+        functools.partial(x_join_kernel, half_x, half_y, x_cells, blocks, "gx", x_ranks, x_rows),
         [
-            near((y_ranks * y_rows, LANES)),
+            near((y_rows, LANES)),
             near((2, weight_rows(y_count), LANES)),
             near((FIELDS, source_rows(y_count), LANES)),
         ],
-        [(x_ranks * spaced(x_rows), LANES), (y_rows, LANES)],
+        [(x_ranks * spaced(x_rows), LANES)],
         "x_join",
     )(received, x_weights, x_pushed, *args[1:])
-    received = exchange(message, y_ranks, "gy")
+    layout, chips = exchange_chips(message, y_ranks, "gy")
     (updated,) = call(
-        functools.partial(y_join_kernel, half_y, x_cells, blocks, "gy", y_ranks, y_rows),
+        functools.partial(y_join_kernel, half_y, x_cells, blocks, "gy", y_ranks, y_rows, layout),
         [far(sizes[0])],
         [(y_ranks * spaced(y_rows), LANES), sizes[0], pltpu.SemaphoreType.DMA((FIELDS,))], "y_join",
         out_specs=[pl.BlockSpec(memory_space=pltpu.HBM)],
-    )(received, y_weights, y_pushed)
+    )(*chips, y_weights, y_pushed)
     return untiles(updated, fields.shape)
 
 

time: 31.4 us -> 29.2 us (0.930)
  blocking collectives: 27.5 us -> 16.7 us
  starting transfers between devices: 0 us -> 6.87 us
  waiting for transfers between devices: 0 us -> 1.76 us
    all_to_all x2 -> x1, blocking collectives: 27.5 us -> 16.7 us  [exchange(): return lax.all_to_all(flat, axis, 0, 0, tiled=True).reshape(-1, LANES)]
    ppermute x0 -> x5, starting transfers between devices: none -> 6.87 us  [send(): return lax.ppermute(array, axis, [(i, i ^ step) for i in range(ranks)])]
    ppermute x0 -> x5, waiting for transfers between devices: none -> 1.76 us  [send(): return lax.ppermute(array, axis, [(i, i ^ step) for i in range(ranks)])]
  transfers between devices with their start and end apart: 0 -> 5, of which waited for: 0 -> 3; matrix products, arithmetic and copies ran while one was open for 0% -> 0% of each run, Pallas kernels for 0% -> 0%
where the time goes in v4:
time: 29.2 us; the launch traced here: 29 us
  blocking collectives  16.7 us (57%)
  starting transfers between devices  6.87 us (24%)
  Pallas kernels  3.64 us (12%)
  waiting for transfers between devices  1.76 us (6%)
    all_to_all x1, blocking collectives, exchange(): return lax.all_to_all(flat, axis, 0, 0, tiled=True).reshape(-1, LANES)  16.7 us
    ppermute x5, starting transfers between devices, send(): return lax.ppermute(array, axis, [(i, i ^ step) for i in range(ranks)])  6.87 us
    ppermute x5, waiting for transfers between devices, send(): return lax.ppermute(array, axis, [(i, i ^ step) for i in range(ranks)])  1.76 us
    pallas_call x1, Pallas kernels, on_device(): call(functools.partial(x_ends_kernel, half_x, x_cells, blocks, x_ranks, x...  1.55 us
    pallas_call x1, Pallas kernels, on_device(): call(functools.partial(y_join_kernel, half_y, x_cells, blocks, 'gy', y_ra...  1.16 us
    pallas_call x1, Pallas kernels, on_device(): call(functools.partial(x_join_kernel, half_x, half_y, x_cells, blocks, 'g...  0.93 us
  transfers between devices with their start and end apart: 5, of which 3 were waited for; matrix products, arithmetic and copies ran while one was open for 0% of the time, Pallas kernels for 0%

profile of v4, /device:TPU:1, one launch (start us, length us, event | category | flops | bytes accessed | tf_op | source)
XLA Modules:
  0.0 29.0 jit_solution(5251521188771498628)
XLA Ops:
  0.0 1.6 %x_ends.1 = (f32[576,128]{1,0:T(8,128)S(1)}, f32[2,2,320,128]{3,2,1,0:T(8,128)S(1)}, f32[4,2,160,128]{3,2,1,0:T(8,128)S(1)}) custom-call(f32[1024,128]{1,0:T(8,128)} %bitcast.28, f32[256,128]{1,0:T(8,128)} %bitcast.23, f32[256,128]{1,0:T(8,128)} %bitcast.25), custom_call_target="tpu_custom_call" | custom-call | tf_op jit(solution)/shard_map/x_ends/pallas_call | solution.py:476
  1.6 0.0 copy-start
  1.6 0.0 copy-start.1
  1.6 16.7 %all_to_all.5 = f32[16,1,4608]{2,1,0:T(1,128)S(1)} all-to-all(f32[16,1,4608]{2,1,0:T(1,128)S(1)} %bitcast.27), channel_id=1, replica_groups=mesh['gx'=16,'gy'=8] {'gx'}, dimensions={0} | all-to-all | bytes 589824 | tf_op jit(solution)/shard_map/all_to_all | solution.py:444
  18.2 0.0 copy-done
  18.2 0.0 copy-done.1
  18.2 0.9 %x_join.1 = (f32[18,128]{1,0:T(8,128)S(1)}, f32[2,576,128]{2,1,0:T(8,128)S(1)}, f32[4,288,128]{2,1,0:T(8,128)S(1)}) custom-call(f32[576,128]{1,0:T(8,128)S(1)} %bitcast.22, f32[2,2,320,128]{3,2,1,0:T(8,128)S(1)} %get-tuple-element.12.x_weights, f32[4,2,160,128]{3,2,1,0:T(8,128)S(1)} %get-tuple-element.13.x_pushed, f32[256,128]{1,0:T(8,128)S(1)} %bitcast.24, ...), custom_call_target="tpu_custom_call" | custom-call | tf_op jit(solution)/shard_map/x_join/pallas_call | solution.py:487
  19.2 1.9 %collective-permute-start = (f32[18,128]{1,0:T(8,128)S(1)}, f32[18,128]{1,0:T(8,128)S(1)}, u32[]{:S(2)}, u32[]{:S(2)}) collective-permute-start(f32[18,128]{1,0:T(8,128)S(1)} %get-tuple-element.14), channel_id=1, source_target_pairs={{0,1},{1,0},{2,3},{3,2},{4,5},{5,4},{6,7},{7,6},{8,9},{9,8},{10,11... | collective-permute-start | bytes 27656 | tf_op jit(solution)/shard_map/ppermute | solution.py:449
  21.1 2.8 %collective-permute-start.3 = (f32[18,128]{1,0:T(8,128)S(1)}, f32[18,128]{1,0:T(8,128)S(1)}, u32[]{:S(2)}, u32[]{:S(2)}) collective-permute-start(f32[18,128]{1,0:T(8,128)S(1)} %get-tuple-element.14), channel_id=1, source_target_pairs={{0,4},{1,5},{2,6},{3,7},{4,0},{5,1},{6,2},{7,3},{8,12},{9,13},{10,... | collective-permute-start | bytes 27656 | tf_op jit(solution)/shard_map/ppermute | solution.py:449
  23.9 0.0 collective-permute-done
  23.9 0.9 %collective-permute-start.2 = (f32[36,128]{1,0:T(8,128)S(1)}, f32[36,128]{1,0:T(8,128)S(1)}, u32[]{:S(2)}, u32[]{:S(2)}) collective-permute-start(f32[36,128]{1,0:T(8,128)S(1)} %pad_maximum_fusion.refs_0_), channel_id=1, source_target_pairs={{0,6},{1,7},{2,4},{3,5},{4,2},{5,3},{6,0},{7,1},{8,14},{9,15},{10,... | collective-permute-start | bytes 55304 | tf_op jit(solution)/shard_map/ppermute | solution.py:449
  24.8 0.0 collective-permute-start.1
  24.8 0.3 %collective-permute-done.3.refs_3_ = f32[18,128]{1,0:T(8,128)S(1)} collective-permute-done((f32[18,128]{1,0:T(8,128)S(1)}, f32[18,128]{1,0:T(8,128)S(1)}, u32[]{:S(2)}, u32[]{:S(2)}) %collective-permute-start.3) | collective-permute-done | bytes 9248 | tf_op jit(solution)/shard_map/ppermute | solution.py:449
  25.2 1.2 %collective-permute-start.4 = (f32[18,128]{1,0:T(8,128)S(1)}, f32[18,128]{1,0:T(8,128)S(1)}, u32[]{:S(2)}, u32[]{:S(2)}) collective-permute-start(f32[18,128]{1,0:T(8,128)S(1)} %collective-permute-done.3.refs_3_), channel_id=1, source_target_pairs={{0,1},{1,0},{2,3},{3,2},{4,5},{5,4},{6,7},{7,6},{8,9},{9,8},{10,11... | collective-permute-start | bytes 27656 | tf_op jit(solution)/shard_map/ppermute | solution.py:449
  26.4 0.8 %collective-permute-done.4.refs_4_ = f32[18,128]{1,0:T(8,128)S(1)} collective-permute-done((f32[18,128]{1,0:T(8,128)S(1)}, f32[18,128]{1,0:T(8,128)S(1)}, u32[]{:S(2)}, u32[]{:S(2)}) %collective-permute-start.4) | collective-permute-done | bytes 9248 | tf_op jit(solution)/shard_map/ppermute | solution.py:449
  27.2 0.6 %collective-permute-done.2.refs_2_ = f32[36,128]{1,0:T(8,128)S(1)} collective-permute-done((f32[36,128]{1,0:T(8,128)S(1)}, f32[36,128]{1,0:T(8,128)S(1)}, u32[]{:S(2)}, u32[]{:S(2)}) %collective-permute-start.2) | collective-permute-done | bytes 18464 | tf_op jit(solution)/shard_map/ppermute | solution.py:449
  27.8 0.0 collective-permute-done.1.refs_1_
  27.8 1.2 %y_join.1 = f32[1024,128]{1,0:T(8,128)} custom-call(f32[36,128]{1,0:T(8,128)S(1)} %pad_maximum_fusion.refs_0_, f32[36,128]{1,0:T(8,128)S(1)} %collective-permute-done.1.refs_1_, f32[36,128]{1,0:T(8,128)S(1)} %collective-permute-done.2.refs_2_, f32[18,128]{1,0:T(8,128)S(1)} %collective-permute-done.3.refs_3_, f32[18,128]{1,0:T(8,128)S(1)} %collective-permute-done.4.refs_4_, ...), custom_call_target="tpu_custom_call" | custom-call | tf_op jit(solution)/shard_map/y_join/pallas_call | solution.py:498
  (1 shorter events, 0.0 us)
Async XLA Ops:
  1.6 16.7 %copy-start = (f32[1,128,256]{2,1,0:T(8,128)S(1)}, f32[1,128,256]{2,1,0:T(8,128)}, u32[]{:S(2)}) copy-start(f32[1,128,256]{2,1,0:T(8,128)} %param.4) | copy-start | bytes 393220
  1.6 16.7 %copy-start.1 = (f32[1,128,256]{2,1,0:T(8,128)S(1)}, f32[1,128,256]{2,1,0:T(8,128)}, u32[]{:S(2)}) copy-start(f32[1,128,256]{2,1,0:T(8,128)} %param.5) | copy-start | bytes 393220
  19.2 4.7 %collective-permute-start = (f32[18,128]{1,0:T(8,128)S(1)}, f32[18,128]{1,0:T(8,128)S(1)}, u32[]{:S(2)}, u32[]{:S(2)}) collective-permute-start(f32[18,128]{1,0:T(8,128)S(1)} %get-tuple-element.14), channel_id=1, source_target_pairs={{0,1},{1,0},{2,3},{3,2},{4,5},{5,4},{6,7},{7,6},{8,9},{9,8},{10,11... | collective-permute-start | bytes 27656 | tf_op jit(solution)/shard_map/ppermute | solution.py:449
  21.1 4.1 %collective-permute-start.3 = (f32[18,128]{1,0:T(8,128)S(1)}, f32[18,128]{1,0:T(8,128)S(1)}, u32[]{:S(2)}, u32[]{:S(2)}) collective-permute-start(f32[18,128]{1,0:T(8,128)S(1)} %get-tuple-element.14), channel_id=1, source_target_pairs={{0,4},{1,5},{2,6},{3,7},{4,0},{5,1},{6,2},{7,3},{8,12},{9,13},{10,... | collective-permute-start | bytes 27656 | tf_op jit(solution)/shard_map/ppermute | solution.py:449
  23.9 3.9 %collective-permute-start.2 = (f32[36,128]{1,0:T(8,128)S(1)}, f32[36,128]{1,0:T(8,128)S(1)}, u32[]{:S(2)}, u32[]{:S(2)}) collective-permute-start(f32[36,128]{1,0:T(8,128)S(1)} %pad_maximum_fusion.refs_0_), channel_id=1, source_target_pairs={{0,6},{1,7},{2,4},{3,5},{4,2},{5,3},{6,0},{7,1},{8,14},{9,15},{10,... | collective-permute-start | bytes 55304 | tf_op jit(solution)/shard_map/ppermute | solution.py:449
  24.8 3.0 %collective-permute-start.1 = (f32[36,128]{1,0:T(8,128)S(1)}, f32[36,128]{1,0:T(8,128)S(1)}, u32[]{:S(2)}, u32[]{:S(2)}) collective-permute-start(f32[36,128]{1,0:T(8,128)S(1)} %pad_maximum_fusion.refs_0_), channel_id=1, source_target_pairs={{0,2},{1,3},{2,0},{3,1},{4,6},{5,7},{6,4},{7,5},{8,10},{9,11},{10,... | collective-permute-start | bytes 55304 | tf_op jit(solution)/shard_map/ppermute | solution.py:449
  25.2 2.1 %collective-permute-start.4 = (f32[18,128]{1,0:T(8,128)S(1)}, f32[18,128]{1,0:T(8,128)S(1)}, u32[]{:S(2)}, u32[]{:S(2)}) collective-permute-start(f32[18,128]{1,0:T(8,128)S(1)} %collective-permute-done.3.refs_3_), channel_id=1, source_target_pairs={{0,1},{1,0},{2,3},{3,2},{4,5},{5,4},{6,7},{7,6},{8,9},{9,8},{10,11... | collective-permute-start | bytes 27656 | tf_op jit(solution)/shard_map/ppermute | solution.py:449

commit v5 on v4

--- a/solution.py
+++ b/solution.py
@@ -17,8 +17,7 @@
 
 
 def recip(value):
-    guess = pl.reciprocal(value, approx=True)
-    return guess * (2.0 - value * guess)
+    return pl.reciprocal(value, approx=True)
 
 
 def up(rows, step):
@@ -449,7 +448,7 @@
         return lax.ppermute(array, axis, [(i, i ^ step) for i in range(ranks)])
 
     chips = range(1, ranks // 2)
-    early = chips[2 - 1]
+    early = chips[3 - 1]
     near_chip = send(message, 2 * early)
     other = send(message, 1)
     both = jnp.concatenate([message, other])

time: 29.2 us -> 29.1 us (level)
  transfers between devices with their start and end apart: 5 -> 5, of which waited for: 3 -> 2; matrix products, arithmetic and copies ran while one was open for 0% -> 0% of each run, Pallas kernels for 0% -> 0%
where the time goes in v5:
time: 29.1 us; the launch traced here: 28.9 us
  blocking collectives  16.7 us (57%)
  starting transfers between devices  6.93 us (24%)
  Pallas kernels  3.51 us (12%)
  waiting for transfers between devices  1.73 us (6%)
    all_to_all x1, blocking collectives, exchange(): return lax.all_to_all(flat, axis, 0, 0, tiled=True).reshape(-1, LANES)  16.7 us
    ppermute x5, starting transfers between devices, send(): return lax.ppermute(array, axis, [(i, i ^ step) for i in range(ranks)])  6.93 us
    ppermute x5, waiting for transfers between devices, send(): return lax.ppermute(array, axis, [(i, i ^ step) for i in range(ranks)])  1.73 us
    pallas_call x1, Pallas kernels, on_device(): call(functools.partial(x_ends_kernel, half_x, x_cells, blocks, x_ranks, x...  1.51 us
    pallas_call x1, Pallas kernels, on_device(): call(functools.partial(y_join_kernel, half_y, x_cells, blocks, 'gy', y_ra...  1.15 us
    pallas_call x1, Pallas kernels, on_device(): call(functools.partial(x_join_kernel, half_x, half_y, x_cells, blocks, 'g...  0.86 us
  transfers between devices with their start and end apart: 5, of which 2 were waited for; matrix products, arithmetic and copies ran while one was open for 0% of the time, Pallas kernels for 0%

profile of v5, /device:TPU:1, one launch (start us, length us, event | category | flops | bytes accessed | tf_op | source)
XLA Modules:
  0.0 28.9 jit_solution(15382780928674821660)
XLA Ops:
  0.0 1.5 %x_ends.1 = (f32[576,128]{1,0:T(8,128)S(1)}, f32[2,2,320,128]{3,2,1,0:T(8,128)S(1)}, f32[4,2,160,128]{3,2,1,0:T(8,128)S(1)}) custom-call(f32[1024,128]{1,0:T(8,128)} %bitcast.28, f32[256,128]{1,0:T(8,128)} %bitcast.23, f32[256,128]{1,0:T(8,128)} %bitcast.25), custom_call_target="tpu_custom_call" | custom-call | tf_op jit(solution)/shard_map/x_ends/pallas_call | solution.py:475
  1.5 0.0 copy-start
  1.5 0.0 copy-start.1
  1.5 16.7 %all_to_all.5 = f32[16,1,4608]{2,1,0:T(1,128)S(1)} all-to-all(f32[16,1,4608]{2,1,0:T(1,128)S(1)} %bitcast.27), channel_id=1, replica_groups=mesh['gx'=16,'gy'=8] {'gx'}, dimensions={0} | all-to-all | bytes 589824 | tf_op jit(solution)/shard_map/all_to_all | solution.py:443
  18.2 0.0 copy-done
  18.2 0.0 copy-done.1
  18.2 0.9 %x_join.1 = (f32[18,128]{1,0:T(8,128)S(1)}, f32[2,576,128]{2,1,0:T(8,128)S(1)}, f32[4,288,128]{2,1,0:T(8,128)S(1)}) custom-call(f32[576,128]{1,0:T(8,128)S(1)} %bitcast.22, f32[2,2,320,128]{3,2,1,0:T(8,128)S(1)} %get-tuple-element.12.x_weights, f32[4,2,160,128]{3,2,1,0:T(8,128)S(1)} %get-tuple-element.13.x_pushed, f32[256,128]{1,0:T(8,128)S(1)} %bitcast.24, ...), custom_call_target="tpu_custom_call" | custom-call | tf_op jit(solution)/shard_map/x_join/pallas_call | solution.py:486
  19.1 1.9 %collective-permute-start = (f32[18,128]{1,0:T(8,128)S(1)}, f32[18,128]{1,0:T(8,128)S(1)}, u32[]{:S(2)}, u32[]{:S(2)}) collective-permute-start(f32[18,128]{1,0:T(8,128)S(1)} %get-tuple-element.14), channel_id=1, source_target_pairs={{0,1},{1,0},{2,3},{3,2},{4,5},{5,4},{6,7},{7,6},{8,9},{9,8},{10,11... | collective-permute-start | bytes 27656 | tf_op jit(solution)/shard_map/ppermute | solution.py:448
  21.0 2.5 %collective-permute-start.3 = (f32[18,128]{1,0:T(8,128)S(1)}, f32[18,128]{1,0:T(8,128)S(1)}, u32[]{:S(2)}, u32[]{:S(2)}) collective-permute-start(f32[18,128]{1,0:T(8,128)S(1)} %get-tuple-element.14), channel_id=1, source_target_pairs={{0,6},{1,7},{2,4},{3,5},{4,2},{5,3},{6,0},{7,1},{8,14},{9,15},{10,... | collective-permute-start | bytes 27656 | tf_op jit(solution)/shard_map/ppermute | solution.py:448
  23.5 0.0 collective-permute-done
  23.5 1.1 %collective-permute-start.2 = (f32[36,128]{1,0:T(8,128)S(1)}, f32[36,128]{1,0:T(8,128)S(1)}, u32[]{:S(2)}, u32[]{:S(2)}) collective-permute-start(f32[36,128]{1,0:T(8,128)S(1)} %pad_maximum_fusion.refs_0_), channel_id=1, source_target_pairs={{0,4},{1,5},{2,6},{3,7},{4,0},{5,1},{6,2},{7,3},{8,12},{9,13},{10,... | collective-permute-start | bytes 55304 | tf_op jit(solution)/shard_map/ppermute | solution.py:448
  24.6 0.3 %collective-permute-start.1 = (f32[36,128]{1,0:T(8,128)S(1)}, f32[36,128]{1,0:T(8,128)S(1)}, u32[]{:S(2)}, u32[]{:S(2)}) collective-permute-start(f32[36,128]{1,0:T(8,128)S(1)} %pad_maximum_fusion.refs_0_), channel_id=1, source_target_pairs={{0,2},{1,3},{2,0},{3,1},{4,6},{5,7},{6,4},{7,5},{8,10},{9,11},{10,... | collective-permute-start | bytes 55304 | tf_op jit(solution)/shard_map/ppermute | solution.py:448
  24.9 0.0 collective-permute-done.3.refs_3_
  24.9 1.1 %collective-permute-start.4 = (f32[18,128]{1,0:T(8,128)S(1)}, f32[18,128]{1,0:T(8,128)S(1)}, u32[]{:S(2)}, u32[]{:S(2)}) collective-permute-start(f32[18,128]{1,0:T(8,128)S(1)} %collective-permute-done.3.refs_3_), channel_id=1, source_target_pairs={{0,1},{1,0},{2,3},{3,2},{4,5},{5,4},{6,7},{7,6},{8,9},{9,8},{10,11... | collective-permute-start | bytes 27656 | tf_op jit(solution)/shard_map/ppermute | solution.py:448
  26.0 0.8 %collective-permute-done.4.refs_4_ = f32[18,128]{1,0:T(8,128)S(1)} collective-permute-done((f32[18,128]{1,0:T(8,128)S(1)}, f32[18,128]{1,0:T(8,128)S(1)}, u32[]{:S(2)}, u32[]{:S(2)}) %collective-permute-start.4) | collective-permute-done | bytes 9248 | tf_op jit(solution)/shard_map/ppermute | solution.py:448
  26.8 0.9 %collective-permute-done.2.refs_2_ = f32[36,128]{1,0:T(8,128)S(1)} collective-permute-done((f32[36,128]{1,0:T(8,128)S(1)}, f32[36,128]{1,0:T(8,128)S(1)}, u32[]{:S(2)}, u32[]{:S(2)}) %collective-permute-start.2) | collective-permute-done | bytes 18464 | tf_op jit(solution)/shard_map/ppermute | solution.py:448
  27.7 0.0 collective-permute-done.1.refs_1_
  27.7 1.1 %y_join.1 = f32[1024,128]{1,0:T(8,128)} custom-call(f32[36,128]{1,0:T(8,128)S(1)} %pad_maximum_fusion.refs_0_, f32[36,128]{1,0:T(8,128)S(1)} %collective-permute-done.1.refs_1_, f32[36,128]{1,0:T(8,128)S(1)} %collective-permute-done.2.refs_2_, f32[18,128]{1,0:T(8,128)S(1)} %collective-permute-done.3.refs_3_, f32[18,128]{1,0:T(8,128)S(1)} %collective-permute-done.4.refs_4_, ...), custom_call_target="tpu_custom_call" | custom-call | tf_op jit(solution)/shard_map/y_join/pallas_call | solution.py:497
  (1 shorter events, 0.0 us)
Async XLA Ops:
  1.5 16.7 %copy-start = (f32[1,128,256]{2,1,0:T(8,128)S(1)}, f32[1,128,256]{2,1,0:T(8,128)}, u32[]{:S(2)}) copy-start(f32[1,128,256]{2,1,0:T(8,128)} %param.4) | copy-start | bytes 393220
  1.5 16.7 %copy-start.1 = (f32[1,128,256]{2,1,0:T(8,128)S(1)}, f32[1,128,256]{2,1,0:T(8,128)}, u32[]{:S(2)}) copy-start(f32[1,128,256]{2,1,0:T(8,128)} %param.5) | copy-start | bytes 393220
  19.1 4.4 %collective-permute-start = (f32[18,128]{1,0:T(8,128)S(1)}, f32[18,128]{1,0:T(8,128)S(1)}, u32[]{:S(2)}, u32[]{:S(2)}) collective-permute-start(f32[18,128]{1,0:T(8,128)S(1)} %get-tuple-element.14), channel_id=1, source_target_pairs={{0,1},{1,0},{2,3},{3,2},{4,5},{5,4},{6,7},{7,6},{8,9},{9,8},{10,11... | collective-permute-start | bytes 27656 | tf_op jit(solution)/shard_map/ppermute | solution.py:448
  21.0 3.9 %collective-permute-start.3 = (f32[18,128]{1,0:T(8,128)S(1)}, f32[18,128]{1,0:T(8,128)S(1)}, u32[]{:S(2)}, u32[]{:S(2)}) collective-permute-start(f32[18,128]{1,0:T(8,128)S(1)} %get-tuple-element.14), channel_id=1, source_target_pairs={{0,6},{1,7},{2,4},{3,5},{4,2},{5,3},{6,0},{7,1},{8,14},{9,15},{10,... | collective-permute-start | bytes 27656 | tf_op jit(solution)/shard_map/ppermute | solution.py:448
  23.5 4.2 %collective-permute-start.2 = (f32[36,128]{1,0:T(8,128)S(1)}, f32[36,128]{1,0:T(8,128)S(1)}, u32[]{:S(2)}, u32[]{:S(2)}) collective-permute-start(f32[36,128]{1,0:T(8,128)S(1)} %pad_maximum_fusion.refs_0_), channel_id=1, source_target_pairs={{0,4},{1,5},{2,6},{3,7},{4,0},{5,1},{6,2},{7,3},{8,12},{9,13},{10,... | collective-permute-start | bytes 55304 | tf_op jit(solution)/shard_map/ppermute | solution.py:448
  24.6 3.1 %collective-permute-start.1 = (f32[36,128]{1,0:T(8,128)S(1)}, f32[36,128]{1,0:T(8,128)S(1)}, u32[]{:S(2)}, u32[]{:S(2)}) collective-permute-start(f32[36,128]{1,0:T(8,128)S(1)} %pad_maximum_fusion.refs_0_), channel_id=1, source_target_pairs={{0,2},{1,3},{2,0},{3,1},{4,6},{5,7},{6,4},{7,5},{8,10},{9,11},{10,... | collective-permute-start | bytes 55304 | tf_op jit(solution)/shard_map/ppermute | solution.py:448
  24.9 1.9 %collective-permute-start.4 = (f32[18,128]{1,0:T(8,128)S(1)}, f32[18,128]{1,0:T(8,128)S(1)}, u32[]{:S(2)}, u32[]{:S(2)}) collective-permute-start(f32[18,128]{1,0:T(8,128)S(1)} %collective-permute-done.3.refs_3_), channel_id=1, source_target_pairs={{0,1},{1,0},{2,3},{3,2},{4,5},{5,4},{6,7},{7,6},{8,9},{9,8},{10,11... | collective-permute-start | bytes 27656 | tf_op jit(solution)/shard_map/ppermute | solution.py:448

commit v6 on v5

--- a/solution.py
+++ b/solution.py
@@ -294,9 +294,13 @@
     return rows | 1
 
 
+def slot(device, ranks):
+    return ranks - 1 - device
+
+
 def rotate(received, turned, ranks, rows, rank):
     for k in range(ranks):
-        source = lax.rem(rank + 1 + k, ranks) * rows
+        source = slot(lax.rem(rank + 1 + k, ranks), ranks) * rows
         turned[pl.ds(k * spaced(rows), rows), :] = received[pl.ds(source, rows), :]
 
 
@@ -440,7 +444,8 @@
 
 def exchange(message, ranks, axis):
     flat = message.reshape(ranks, 1, -1)
-    return lax.all_to_all(flat, axis, 0, 0, tiled=True).reshape(-1, LANES)
+    order = sorted(range(ranks), key=lambda device: slot(device, ranks))
+    return lax.all_to_all(flat, axis, 0, 0, tiled=True, axis_index_groups=[order]).reshape(-1, LANES)
 
 
 def exchange_chips(message, ranks, axis):

time: 29.1 us -> 26.5 us (0.911)
  blocking collectives: 16.7 us -> 14.3 us
  starting transfers between devices: 6.93 us -> 6.63 us
    all_to_all x1, blocking collectives: 16.7 us -> 14.3 us  [exchange(): lax.all_to_all(flat, axis, 0, 0, tiled=True, axis_index_groups=[order])]
    ppermute x5, starting transfers between devices: 6.93 us -> 6.63 us  [send(): return lax.ppermute(array, axis, [(i, i ^ step) for i in range(ranks)])]
where the time goes in v6:
time: 26.5 us; the launch traced here: 26.2 us
  blocking collectives  14.3 us (54%)
  starting transfers between devices  6.63 us (25%)
  Pallas kernels  3.51 us (13%)
  waiting for transfers between devices  1.73 us (7%)
    all_to_all x1, blocking collectives, exchange(): lax.all_to_all(flat, axis, 0, 0, tiled=True, axis_index_groups=[order])  14.3 us
    ppermute x5, starting transfers between devices, send(): return lax.ppermute(array, axis, [(i, i ^ step) for i in range(ranks)])  6.63 us
    ppermute x5, waiting for transfers between devices, send(): return lax.ppermute(array, axis, [(i, i ^ step) for i in range(ranks)])  1.73 us
    pallas_call x1, Pallas kernels, on_device(): call(functools.partial(x_ends_kernel, half_x, x_cells, blocks, x_ranks, x...  1.51 us
    pallas_call x1, Pallas kernels, on_device(): call(functools.partial(y_join_kernel, half_y, x_cells, blocks, 'gy', y_ra...  1.15 us
    pallas_call x1, Pallas kernels, on_device(): call(functools.partial(x_join_kernel, half_x, half_y, x_cells, blocks, 'g...  0.85 us
  transfers between devices with their start and end apart: 5, of which 2 were waited for; matrix products, arithmetic and copies ran while one was open for 0% of the time, Pallas kernels for 0%

profile of v6, /device:TPU:1, one launch (start us, length us, event | category | flops | bytes accessed | tf_op | source)
XLA Modules:
  0.0 26.2 jit_solution(4671499363970971659)
XLA Ops:
  0.0 1.5 %x_ends.1 = (f32[576,128]{1,0:T(8,128)S(1)}, f32[2,2,320,128]{3,2,1,0:T(8,128)S(1)}, f32[4,2,160,128]{3,2,1,0:T(8,128)S(1)}) custom-call(f32[1024,128]{1,0:T(8,128)} %bitcast.28, f32[256,128]{1,0:T(8,128)} %bitcast.23, f32[256,128]{1,0:T(8,128)} %bitcast.25), custom_call_target="tpu_custom_call" | custom-call | tf_op jit(solution)/shard_map/x_ends/pallas_call | solution.py:480
  1.5 0.0 copy-start
  1.5 0.0 copy-start.1
  1.5 14.3 %all_to_all.5 = f32[16,1,4608]{2,1,0:T(1,128)S(1)} all-to-all(f32[16,1,4608]{2,1,0:T(1,128)S(1)} %bitcast.27), channel_id=1, replica_groups={{120,112,104,96,88,80,72,64,56,48,40,32,24,16,8,0},{121,113,105,97,89,8..., dimensions={0} | all-to-all | bytes 589824 | tf_op jit(solution)/shard_map/all_to_all | solution.py:448
  15.8 0.0 copy-done
  15.8 0.0 copy-done.1
  15.9 0.9 %x_join.1 = (f32[18,128]{1,0:T(8,128)S(1)}, f32[2,576,128]{2,1,0:T(8,128)S(1)}, f32[4,288,128]{2,1,0:T(8,128)S(1)}) custom-call(f32[576,128]{1,0:T(8,128)S(1)} %bitcast.22, f32[2,2,320,128]{3,2,1,0:T(8,128)S(1)} %get-tuple-element.12.x_weights, f32[4,2,160,128]{3,2,1,0:T(8,128)S(1)} %get-tuple-element.13.x_pushed, f32[256,128]{1,0:T(8,128)S(1)} %bitcast.24, ...), custom_call_target="tpu_custom_call" | custom-call | tf_op jit(solution)/shard_map/x_join/pallas_call | solution.py:491
  16.7 1.7 %collective-permute-start = (f32[18,128]{1,0:T(8,128)S(1)}, f32[18,128]{1,0:T(8,128)S(1)}, u32[]{:S(2)}, u32[]{:S(2)}) collective-permute-start(f32[18,128]{1,0:T(8,128)S(1)} %get-tuple-element.14), channel_id=1, source_target_pairs={{0,1},{1,0},{2,3},{3,2},{4,5},{5,4},{6,7},{7,6},{8,9},{9,8},{10,11... | collective-permute-start | bytes 27656 | tf_op jit(solution)/shard_map/ppermute | solution.py:453
  18.4 2.5 %collective-permute-start.3 = (f32[18,128]{1,0:T(8,128)S(1)}, f32[18,128]{1,0:T(8,128)S(1)}, u32[]{:S(2)}, u32[]{:S(2)}) collective-permute-start(f32[18,128]{1,0:T(8,128)S(1)} %get-tuple-element.14), channel_id=1, source_target_pairs={{0,6},{1,7},{2,4},{3,5},{4,2},{5,3},{6,0},{7,1},{8,14},{9,15},{10,... | collective-permute-start | bytes 27656 | tf_op jit(solution)/shard_map/ppermute | solution.py:453
  20.9 0.0 collective-permute-done
  20.9 1.1 %collective-permute-start.2 = (f32[36,128]{1,0:T(8,128)S(1)}, f32[36,128]{1,0:T(8,128)S(1)}, u32[]{:S(2)}, u32[]{:S(2)}) collective-permute-start(f32[36,128]{1,0:T(8,128)S(1)} %pad_maximum_fusion.refs_0_), channel_id=1, source_target_pairs={{0,4},{1,5},{2,6},{3,7},{4,0},{5,1},{6,2},{7,3},{8,12},{9,13},{10,... | collective-permute-start | bytes 55304 | tf_op jit(solution)/shard_map/ppermute | solution.py:453
  22.0 0.3 %collective-permute-start.1 = (f32[36,128]{1,0:T(8,128)S(1)}, f32[36,128]{1,0:T(8,128)S(1)}, u32[]{:S(2)}, u32[]{:S(2)}) collective-permute-start(f32[36,128]{1,0:T(8,128)S(1)} %pad_maximum_fusion.refs_0_), channel_id=1, source_target_pairs={{0,2},{1,3},{2,0},{3,1},{4,6},{5,7},{6,4},{7,5},{8,10},{9,11},{10,... | collective-permute-start | bytes 55304 | tf_op jit(solution)/shard_map/ppermute | solution.py:453
  22.3 0.0 collective-permute-done.3.refs_3_
  22.3 1.1 %collective-permute-start.4 = (f32[18,128]{1,0:T(8,128)S(1)}, f32[18,128]{1,0:T(8,128)S(1)}, u32[]{:S(2)}, u32[]{:S(2)}) collective-permute-start(f32[18,128]{1,0:T(8,128)S(1)} %collective-permute-done.3.refs_3_), channel_id=1, source_target_pairs={{0,1},{1,0},{2,3},{3,2},{4,5},{5,4},{6,7},{7,6},{8,9},{9,8},{10,11... | collective-permute-start | bytes 27656 | tf_op jit(solution)/shard_map/ppermute | solution.py:453
  23.4 0.8 %collective-permute-done.4.refs_4_ = f32[18,128]{1,0:T(8,128)S(1)} collective-permute-done((f32[18,128]{1,0:T(8,128)S(1)}, f32[18,128]{1,0:T(8,128)S(1)}, u32[]{:S(2)}, u32[]{:S(2)}) %collective-permute-start.4) | collective-permute-done | bytes 9248 | tf_op jit(solution)/shard_map/ppermute | solution.py:453
  24.2 0.9 %collective-permute-done.2.refs_2_ = f32[36,128]{1,0:T(8,128)S(1)} collective-permute-done((f32[36,128]{1,0:T(8,128)S(1)}, f32[36,128]{1,0:T(8,128)S(1)}, u32[]{:S(2)}, u32[]{:S(2)}) %collective-permute-start.2) | collective-permute-done | bytes 18464 | tf_op jit(solution)/shard_map/ppermute | solution.py:453
  25.1 0.0 collective-permute-done.1.refs_1_
  25.1 1.1 %y_join.1 = f32[1024,128]{1,0:T(8,128)} custom-call(f32[36,128]{1,0:T(8,128)S(1)} %pad_maximum_fusion.refs_0_, f32[36,128]{1,0:T(8,128)S(1)} %collective-permute-done.1.refs_1_, f32[36,128]{1,0:T(8,128)S(1)} %collective-permute-done.2.refs_2_, f32[18,128]{1,0:T(8,128)S(1)} %collective-permute-done.3.refs_3_, f32[18,128]{1,0:T(8,128)S(1)} %collective-permute-done.4.refs_4_, ...), custom_call_target="tpu_custom_call" | custom-call | tf_op jit(solution)/shard_map/y_join/pallas_call | solution.py:502
  (1 shorter events, 0.0 us)
Async XLA Ops:
  1.5 14.3 %copy-start = (f32[1,128,256]{2,1,0:T(8,128)S(1)}, f32[1,128,256]{2,1,0:T(8,128)}, u32[]{:S(2)}) copy-start(f32[1,128,256]{2,1,0:T(8,128)} %param.4) | copy-start | bytes 393220
  1.5 14.3 %copy-start.1 = (f32[1,128,256]{2,1,0:T(8,128)S(1)}, f32[1,128,256]{2,1,0:T(8,128)}, u32[]{:S(2)}) copy-start(f32[1,128,256]{2,1,0:T(8,128)} %param.5) | copy-start | bytes 393220
  16.7 4.1 %collective-permute-start = (f32[18,128]{1,0:T(8,128)S(1)}, f32[18,128]{1,0:T(8,128)S(1)}, u32[]{:S(2)}, u32[]{:S(2)}) collective-permute-start(f32[18,128]{1,0:T(8,128)S(1)} %get-tuple-element.14), channel_id=1, source_target_pairs={{0,1},{1,0},{2,3},{3,2},{4,5},{5,4},{6,7},{7,6},{8,9},{9,8},{10,11... | collective-permute-start | bytes 27656 | tf_op jit(solution)/shard_map/ppermute | solution.py:453
  18.4 3.9 %collective-permute-start.3 = (f32[18,128]{1,0:T(8,128)S(1)}, f32[18,128]{1,0:T(8,128)S(1)}, u32[]{:S(2)}, u32[]{:S(2)}) collective-permute-start(f32[18,128]{1,0:T(8,128)S(1)} %get-tuple-element.14), channel_id=1, source_target_pairs={{0,6},{1,7},{2,4},{3,5},{4,2},{5,3},{6,0},{7,1},{8,14},{9,15},{10,... | collective-permute-start | bytes 27656 | tf_op jit(solution)/shard_map/ppermute | solution.py:453
  20.9 4.2 %collective-permute-start.2 = (f32[36,128]{1,0:T(8,128)S(1)}, f32[36,128]{1,0:T(8,128)S(1)}, u32[]{:S(2)}, u32[]{:S(2)}) collective-permute-start(f32[36,128]{1,0:T(8,128)S(1)} %pad_maximum_fusion.refs_0_), channel_id=1, source_target_pairs={{0,4},{1,5},{2,6},{3,7},{4,0},{5,1},{6,2},{7,3},{8,12},{9,13},{10,... | collective-permute-start | bytes 55304 | tf_op jit(solution)/shard_map/ppermute | solution.py:453
  22.0 3.1 %collective-permute-start.1 = (f32[36,128]{1,0:T(8,128)S(1)}, f32[36,128]{1,0:T(8,128)S(1)}, u32[]{:S(2)}, u32[]{:S(2)}) collective-permute-start(f32[36,128]{1,0:T(8,128)S(1)} %pad_maximum_fusion.refs_0_), channel_id=1, source_target_pairs={{0,2},{1,3},{2,0},{3,1},{4,6},{5,7},{6,4},{7,5},{8,10},{9,11},{10,... | collective-permute-start | bytes 55304 | tf_op jit(solution)/shard_map/ppermute | solution.py:453
  22.3 1.9 %collective-permute-start.4 = (f32[18,128]{1,0:T(8,128)S(1)}, f32[18,128]{1,0:T(8,128)S(1)}, u32[]{:S(2)}, u32[]{:S(2)}) collective-permute-start(f32[18,128]{1,0:T(8,128)S(1)} %collective-permute-done.3.refs_3_), channel_id=1, source_target_pairs={{0,1},{1,0},{2,3},{3,2},{4,5},{5,4},{6,7},{7,6},{8,9},{9,8},{10,11... | collective-permute-start | bytes 27656 | tf_op jit(solution)/shard_map/ppermute | solution.py:453

commit v7 on v5

--- a/solution.py
+++ b/solution.py
@@ -294,10 +294,10 @@
     return rows | 1
 
 
-def rotate(received, turned, ranks, rows, rank):
-    for k in range(ranks):
-        source = lax.rem(rank + 1 + k, ranks) * rows
-        turned[pl.ds(k * spaced(rows), rows), :] = received[pl.ds(source, rows), :]
+def rotate(received, turned, order, rows, rank):
+    for at, device in enumerate(order):
+        k = lax.rem(device + len(order) - 1 - rank, len(order))
+        turned[pl.ds(k * spaced(rows), rows), :] = received[pl.ds(at * rows, rows), :]
 
 
 def place(parts, turned, ranks, rows, rank):
@@ -355,13 +355,14 @@
 
 
 def x_join_kernel(
-    half_x, half_y, x_cells, blocks, axis, ranks, rows,
+    half_x, half_y, x_cells, blocks, axis, order, rows,
     received, x_weights, x_pushed, viscosity, diffusivity, message, weights, pushed,
     turned,
 ):
     rank = lax.axis_index(axis)
     count, y_count = x_cells // SUB, blocks * LANES // SUB
-    rotate(received, turned, ranks, rows, rank)
+    rotate(received, turned, order, rows, rank)
+    ranks = len(order)
     plans = []
     for kind, coef in enumerate((viscosity, diffusivity)):
         coefs = to_cells(jnp.concatenate([load_block(coef, 0, b, x_cells, blocks).T for b in range(blocks)]))
@@ -438,9 +439,13 @@
     return pltpu.HBM(shape, jnp.float32)
 
 
-def exchange(message, ranks, axis):
-    flat = message.reshape(ranks, 1, -1)
-    return lax.all_to_all(flat, axis, 0, 0, tiled=True).reshape(-1, LANES)
+def exchange(message, order, axis):
+    flat = message.reshape(len(order), 1, -1)
+    return lax.all_to_all(flat, axis, 0, 0, tiled=True, axis_index_groups=[list(order)]).reshape(-1, LANES)
+
+
+def first_in_line(ranks, first):
+    return (first, *(device for device in range(ranks) if device != first))
 
 
 def exchange_chips(message, ranks, axis):
@@ -467,6 +472,7 @@
     blocks = y_cells // LANES
     half_x, half_y = 0.5 * float(x_cells * x_cells), 0.5 * float(y_cells * y_cells)
     x_rows, y_rows = QUANTITIES * blocks, QUANTITIES
+    x_order = first_in_line(x_ranks, 10)
     x_count, y_count = x_cells // SUB, y_cells // SUB
     args = [tiles(a) for a in (fields, viscosity, diffusivity)]
     sizes = [a.shape for a in args]
@@ -482,9 +488,9 @@
         [(x_rows, LANES), *sizes, pltpu.SemaphoreType.DMA((2 + FIELDS,))], "x_ends",
         in_specs=[pl.BlockSpec(memory_space=pltpu.HBM)] * 3,
     )(*in_hbm)
-    received = exchange(message, x_ranks, "gx")
+    received = exchange(message, x_order, "gx")
     message, y_weights, y_pushed = call(
-        functools.partial(x_join_kernel, half_x, half_y, x_cells, blocks, "gx", x_ranks, x_rows),
+        functools.partial(x_join_kernel, half_x, half_y, x_cells, blocks, "gx", x_order, x_rows),
         [
             near((y_rows, LANES)),
             near((2, weight_rows(y_count), LANES)),

time: 29.1 us -> 26.2 us (0.900)
  blocking collectives: 16.7 us -> 13.8 us
    all_to_all x1, blocking collectives: 16.7 us -> 13.8 us  [exchange(): lax.all_to_all(flat, axis, 0, 0, tiled=True, axis_index_groups=[list(orde...]
where the time goes in v7:
time: 26.2 us; the launch traced here: 26 us
  blocking collectives  13.8 us (53%)
  starting transfers between devices  6.93 us (26%)
  Pallas kernels  3.51 us (13%)
  waiting for transfers between devices  1.73 us (7%)
    all_to_all x1, blocking collectives, exchange(): lax.all_to_all(flat, axis, 0, 0, tiled=True, axis_index_groups=[list(orde...  13.8 us
    ppermute x5, starting transfers between devices, send(): return lax.ppermute(array, axis, [(i, i ^ step) for i in range(ranks)])  6.93 us
    ppermute x5, waiting for transfers between devices, send(): return lax.ppermute(array, axis, [(i, i ^ step) for i in range(ranks)])  1.73 us
    pallas_call x1, Pallas kernels, on_device(): call(functools.partial(x_ends_kernel, half_x, x_cells, blocks, x_ranks, x...  1.51 us
    pallas_call x1, Pallas kernels, on_device(): call(functools.partial(y_join_kernel, half_y, x_cells, blocks, 'gy', y_ra...  1.15 us
    pallas_call x1, Pallas kernels, on_device(): call(functools.partial(x_join_kernel, half_x, half_y, x_cells, blocks, 'g...  0.85 us
  transfers between devices with their start and end apart: 5, of which 2 were waited for; matrix products, arithmetic and copies ran while one was open for 0% of the time, Pallas kernels for 0%

profile of v7, /device:TPU:1, one launch (start us, length us, event | category | flops | bytes accessed | tf_op | source)
XLA Modules:
  0.0 26.0 jit_solution(15981332921904342912)
XLA Ops:
  0.0 1.5 %x_ends.1 = (f32[576,128]{1,0:T(8,128)S(1)}, f32[2,2,320,128]{3,2,1,0:T(8,128)S(1)}, f32[4,2,160,128]{3,2,1,0:T(8,128)S(1)}) custom-call(f32[1024,128]{1,0:T(8,128)} %bitcast.28, f32[256,128]{1,0:T(8,128)} %bitcast.23, f32[256,128]{1,0:T(8,128)} %bitcast.25), custom_call_target="tpu_custom_call" | custom-call | tf_op jit(solution)/shard_map/x_ends/pallas_call | solution.py:481
  1.5 0.0 copy-start
  1.5 0.0 copy-start.1
  1.5 13.8 %all_to_all.5 = f32[16,1,4608]{2,1,0:T(1,128)S(1)} all-to-all(f32[16,1,4608]{2,1,0:T(1,128)S(1)} %bitcast.27), channel_id=1, replica_groups={{80,0,8,16,24,32,40,48,56,64,72,88,96,104,112,120},{81,1,9,17,25,33,41,..., dimensions={0} | all-to-all | bytes 589824 | tf_op jit(solution)/shard_map/all_to_all | solution.py:444
  15.3 0.0 copy-done
  15.3 0.0 copy-done.1
  15.3 0.9 %x_join.1 = (f32[18,128]{1,0:T(8,128)S(1)}, f32[2,576,128]{2,1,0:T(8,128)S(1)}, f32[4,288,128]{2,1,0:T(8,128)S(1)}) custom-call(f32[576,128]{1,0:T(8,128)S(1)} %bitcast.22, f32[2,2,320,128]{3,2,1,0:T(8,128)S(1)} %get-tuple-element.12.x_weights, f32[4,2,160,128]{3,2,1,0:T(8,128)S(1)} %get-tuple-element.13.x_pushed, f32[256,128]{1,0:T(8,128)S(1)} %bitcast.24, ...), custom_call_target="tpu_custom_call" | custom-call | tf_op jit(solution)/shard_map/x_join/pallas_call | solution.py:492
  16.2 1.9 %collective-permute-start = (f32[18,128]{1,0:T(8,128)S(1)}, f32[18,128]{1,0:T(8,128)S(1)}, u32[]{:S(2)}, u32[]{:S(2)}) collective-permute-start(f32[18,128]{1,0:T(8,128)S(1)} %get-tuple-element.14), channel_id=1, source_target_pairs={{0,1},{1,0},{2,3},{3,2},{4,5},{5,4},{6,7},{7,6},{8,9},{9,8},{10,11... | collective-permute-start | bytes 27656 | tf_op jit(solution)/shard_map/ppermute | solution.py:453
  18.1 2.5 %collective-permute-start.3 = (f32[18,128]{1,0:T(8,128)S(1)}, f32[18,128]{1,0:T(8,128)S(1)}, u32[]{:S(2)}, u32[]{:S(2)}) collective-permute-start(f32[18,128]{1,0:T(8,128)S(1)} %get-tuple-element.14), channel_id=1, source_target_pairs={{0,6},{1,7},{2,4},{3,5},{4,2},{5,3},{6,0},{7,1},{8,14},{9,15},{10,... | collective-permute-start | bytes 27656 | tf_op jit(solution)/shard_map/ppermute | solution.py:453
  20.6 0.0 collective-permute-done
  20.6 1.1 %collective-permute-start.2 = (f32[36,128]{1,0:T(8,128)S(1)}, f32[36,128]{1,0:T(8,128)S(1)}, u32[]{:S(2)}, u32[]{:S(2)}) collective-permute-start(f32[36,128]{1,0:T(8,128)S(1)} %pad_maximum_fusion.refs_0_), channel_id=1, source_target_pairs={{0,4},{1,5},{2,6},{3,7},{4,0},{5,1},{6,2},{7,3},{8,12},{9,13},{10,... | collective-permute-start | bytes 55304 | tf_op jit(solution)/shard_map/ppermute | solution.py:453
  21.7 0.3 %collective-permute-start.1 = (f32[36,128]{1,0:T(8,128)S(1)}, f32[36,128]{1,0:T(8,128)S(1)}, u32[]{:S(2)}, u32[]{:S(2)}) collective-permute-start(f32[36,128]{1,0:T(8,128)S(1)} %pad_maximum_fusion.refs_0_), channel_id=1, source_target_pairs={{0,2},{1,3},{2,0},{3,1},{4,6},{5,7},{6,4},{7,5},{8,10},{9,11},{10,... | collective-permute-start | bytes 55304 | tf_op jit(solution)/shard_map/ppermute | solution.py:453
  22.0 0.0 collective-permute-done.3.refs_3_
  22.0 1.1 %collective-permute-start.4 = (f32[18,128]{1,0:T(8,128)S(1)}, f32[18,128]{1,0:T(8,128)S(1)}, u32[]{:S(2)}, u32[]{:S(2)}) collective-permute-start(f32[18,128]{1,0:T(8,128)S(1)} %collective-permute-done.3.refs_3_), channel_id=1, source_target_pairs={{0,1},{1,0},{2,3},{3,2},{4,5},{5,4},{6,7},{7,6},{8,9},{9,8},{10,11... | collective-permute-start | bytes 27656 | tf_op jit(solution)/shard_map/ppermute | solution.py:453
  23.1 0.8 %collective-permute-done.4.refs_4_ = f32[18,128]{1,0:T(8,128)S(1)} collective-permute-done((f32[18,128]{1,0:T(8,128)S(1)}, f32[18,128]{1,0:T(8,128)S(1)}, u32[]{:S(2)}, u32[]{:S(2)}) %collective-permute-start.4) | collective-permute-done | bytes 9248 | tf_op jit(solution)/shard_map/ppermute | solution.py:453
  23.9 0.9 %collective-permute-done.2.refs_2_ = f32[36,128]{1,0:T(8,128)S(1)} collective-permute-done((f32[36,128]{1,0:T(8,128)S(1)}, f32[36,128]{1,0:T(8,128)S(1)}, u32[]{:S(2)}, u32[]{:S(2)}) %collective-permute-start.2) | collective-permute-done | bytes 18464 | tf_op jit(solution)/shard_map/ppermute | solution.py:453
  24.8 0.0 collective-permute-done.1.refs_1_
  24.8 1.1 %y_join.1 = f32[1024,128]{1,0:T(8,128)} custom-call(f32[36,128]{1,0:T(8,128)S(1)} %pad_maximum_fusion.refs_0_, f32[36,128]{1,0:T(8,128)S(1)} %collective-permute-done.1.refs_1_, f32[36,128]{1,0:T(8,128)S(1)} %collective-permute-done.2.refs_2_, f32[18,128]{1,0:T(8,128)S(1)} %collective-permute-done.3.refs_3_, f32[18,128]{1,0:T(8,128)S(1)} %collective-permute-done.4.refs_4_, ...), custom_call_target="tpu_custom_call" | custom-call | tf_op jit(solution)/shard_map/y_join/pallas_call | solution.py:503
  (1 shorter events, 0.0 us)
Async XLA Ops:
  1.5 13.8 %copy-start = (f32[1,128,256]{2,1,0:T(8,128)S(1)}, f32[1,128,256]{2,1,0:T(8,128)}, u32[]{:S(2)}) copy-start(f32[1,128,256]{2,1,0:T(8,128)} %param.4) | copy-start | bytes 393220
  1.5 13.8 %copy-start.1 = (f32[1,128,256]{2,1,0:T(8,128)S(1)}, f32[1,128,256]{2,1,0:T(8,128)}, u32[]{:S(2)}) copy-start(f32[1,128,256]{2,1,0:T(8,128)} %param.5) | copy-start | bytes 393220
  16.2 4.4 %collective-permute-start = (f32[18,128]{1,0:T(8,128)S(1)}, f32[18,128]{1,0:T(8,128)S(1)}, u32[]{:S(2)}, u32[]{:S(2)}) collective-permute-start(f32[18,128]{1,0:T(8,128)S(1)} %get-tuple-element.14), channel_id=1, source_target_pairs={{0,1},{1,0},{2,3},{3,2},{4,5},{5,4},{6,7},{7,6},{8,9},{9,8},{10,11... | collective-permute-start | bytes 27656 | tf_op jit(solution)/shard_map/ppermute | solution.py:453
  18.1 3.9 %collective-permute-start.3 = (f32[18,128]{1,0:T(8,128)S(1)}, f32[18,128]{1,0:T(8,128)S(1)}, u32[]{:S(2)}, u32[]{:S(2)}) collective-permute-start(f32[18,128]{1,0:T(8,128)S(1)} %get-tuple-element.14), channel_id=1, source_target_pairs={{0,6},{1,7},{2,4},{3,5},{4,2},{5,3},{6,0},{7,1},{8,14},{9,15},{10,... | collective-permute-start | bytes 27656 | tf_op jit(solution)/shard_map/ppermute | solution.py:453
  20.6 4.2 %collective-permute-start.2 = (f32[36,128]{1,0:T(8,128)S(1)}, f32[36,128]{1,0:T(8,128)S(1)}, u32[]{:S(2)}, u32[]{:S(2)}) collective-permute-start(f32[36,128]{1,0:T(8,128)S(1)} %pad_maximum_fusion.refs_0_), channel_id=1, source_target_pairs={{0,4},{1,5},{2,6},{3,7},{4,0},{5,1},{6,2},{7,3},{8,12},{9,13},{10,... | collective-permute-start | bytes 55304 | tf_op jit(solution)/shard_map/ppermute | solution.py:453
  21.7 3.1 %collective-permute-start.1 = (f32[36,128]{1,0:T(8,128)S(1)}, f32[36,128]{1,0:T(8,128)S(1)}, u32[]{:S(2)}, u32[]{:S(2)}) collective-permute-start(f32[36,128]{1,0:T(8,128)S(1)} %pad_maximum_fusion.refs_0_), channel_id=1, source_target_pairs={{0,2},{1,3},{2,0},{3,1},{4,6},{5,7},{6,4},{7,5},{8,10},{9,11},{10,... | collective-permute-start | bytes 55304 | tf_op jit(solution)/shard_map/ppermute | solution.py:453
  22.0 1.9 %collective-permute-start.4 = (f32[18,128]{1,0:T(8,128)S(1)}, f32[18,128]{1,0:T(8,128)S(1)}, u32[]{:S(2)}, u32[]{:S(2)}) collective-permute-start(f32[18,128]{1,0:T(8,128)S(1)} %collective-permute-done.3.refs_3_), channel_id=1, source_target_pairs={{0,1},{1,0},{2,3},{3,2},{4,5},{5,4},{6,7},{7,6},{8,9},{9,8},{10,11... | collective-permute-start | bytes 27656 | tf_op jit(solution)/shard_map/ppermute | solution.py:453

commit v8 on v7

--- a/solution.py
+++ b/solution.py
@@ -444,8 +444,7 @@
     return lax.all_to_all(flat, axis, 0, 0, tiled=True, axis_index_groups=[list(order)]).reshape(-1, LANES)
 
 
-def first_in_line(ranks, first):
-    return (first, *(device for device in range(ranks) if device != first))
+X_ORDER = (10, 3, 1, 2, 0, 4, 5, 6, 7, 8, 9, 11, 12, 13, 14, 15)
 
 
 def exchange_chips(message, ranks, axis):
@@ -472,7 +471,8 @@
     blocks = y_cells // LANES
     half_x, half_y = 0.5 * float(x_cells * x_cells), 0.5 * float(y_cells * y_cells)
     x_rows, y_rows = QUANTITIES * blocks, QUANTITIES
-    x_order = first_in_line(x_ranks, 10)
+    x_order = X_ORDER
+    assert sorted(x_order) == list(range(x_ranks))
     x_count, y_count = x_cells // SUB, y_cells // SUB
     args = [tiles(a) for a in (fields, viscosity, diffusivity)]
     sizes = [a.shape for a in args]

time: 26.2 us -> 26 us (level)
  no operation moved by 1% of the time
where the time goes in v8:
time: 26 us; the launch traced here: 25.8 us
  blocking collectives  13.8 us (53%)
  starting transfers between devices  6.7 us (26%)
  Pallas kernels  3.51 us (14%)
  waiting for transfers between devices  1.73 us (7%)
    all_to_all x1, blocking collectives, exchange(): lax.all_to_all(flat, axis, 0, 0, tiled=True, axis_index_groups=[list(orde...  13.8 us
    ppermute x5, starting transfers between devices, send(): return lax.ppermute(array, axis, [(i, i ^ step) for i in range(ranks)])  6.7 us
    ppermute x5, waiting for transfers between devices, send(): return lax.ppermute(array, axis, [(i, i ^ step) for i in range(ranks)])  1.73 us
    pallas_call x1, Pallas kernels, on_device(): call(functools.partial(x_ends_kernel, half_x, x_cells, blocks, x_ranks, x...  1.51 us
    pallas_call x1, Pallas kernels, on_device(): call(functools.partial(y_join_kernel, half_y, x_cells, blocks, 'gy', y_ra...  1.15 us
    pallas_call x1, Pallas kernels, on_device(): call(functools.partial(x_join_kernel, half_x, half_y, x_cells, blocks, 'g...  0.85 us
  transfers between devices with their start and end apart: 5, of which 2 were waited for; matrix products, arithmetic and copies ran while one was open for 0% of the time, Pallas kernels for 0%

profile of v8, /device:TPU:1, one launch (start us, length us, event | category | flops | bytes accessed | tf_op | source)
XLA Modules:
  0.0 25.8 jit_solution(17750299919103788669)
XLA Ops:
  0.0 1.5 %x_ends.1 = (f32[576,128]{1,0:T(8,128)S(1)}, f32[2,2,320,128]{3,2,1,0:T(8,128)S(1)}, f32[4,2,160,128]{3,2,1,0:T(8,128)S(1)}) custom-call(f32[1024,128]{1,0:T(8,128)} %bitcast.28, f32[256,128]{1,0:T(8,128)} %bitcast.23, f32[256,128]{1,0:T(8,128)} %bitcast.25), custom_call_target="tpu_custom_call" | custom-call | tf_op jit(solution)/shard_map/x_ends/pallas_call | solution.py:481
  1.5 0.0 copy-start
  1.5 0.0 copy-start.1
  1.5 13.8 %all_to_all.5 = f32[16,1,4608]{2,1,0:T(1,128)S(1)} all-to-all(f32[16,1,4608]{2,1,0:T(1,128)S(1)} %bitcast.27), channel_id=1, replica_groups={{80,24,8,16,0,32,40,48,56,64,72,88,96,104,112,120},{81,25,9,17,1,33,41,..., dimensions={0} | all-to-all | bytes 589824 | tf_op jit(solution)/shard_map/all_to_all | solution.py:444
  15.3 0.0 copy-done
  15.3 0.0 copy-done.1
  15.3 0.9 %x_join.1 = (f32[18,128]{1,0:T(8,128)S(1)}, f32[2,576,128]{2,1,0:T(8,128)S(1)}, f32[4,288,128]{2,1,0:T(8,128)S(1)}) custom-call(f32[576,128]{1,0:T(8,128)S(1)} %bitcast.22, f32[2,2,320,128]{3,2,1,0:T(8,128)S(1)} %get-tuple-element.12.x_weights, f32[4,2,160,128]{3,2,1,0:T(8,128)S(1)} %get-tuple-element.13.x_pushed, f32[256,128]{1,0:T(8,128)S(1)} %bitcast.24, ...), custom_call_target="tpu_custom_call" | custom-call | tf_op jit(solution)/shard_map/x_join/pallas_call | solution.py:492
  16.2 1.7 %collective-permute-start = (f32[18,128]{1,0:T(8,128)S(1)}, f32[18,128]{1,0:T(8,128)S(1)}, u32[]{:S(2)}, u32[]{:S(2)}) collective-permute-start(f32[18,128]{1,0:T(8,128)S(1)} %get-tuple-element.14), channel_id=1, source_target_pairs={{0,1},{1,0},{2,3},{3,2},{4,5},{5,4},{6,7},{7,6},{8,9},{9,8},{10,11... | collective-permute-start | bytes 27656 | tf_op jit(solution)/shard_map/ppermute | solution.py:452
  17.9 2.5 %collective-permute-start.3 = (f32[18,128]{1,0:T(8,128)S(1)}, f32[18,128]{1,0:T(8,128)S(1)}, u32[]{:S(2)}, u32[]{:S(2)}) collective-permute-start(f32[18,128]{1,0:T(8,128)S(1)} %get-tuple-element.14), channel_id=1, source_target_pairs={{0,6},{1,7},{2,4},{3,5},{4,2},{5,3},{6,0},{7,1},{8,14},{9,15},{10,... | collective-permute-start | bytes 27656 | tf_op jit(solution)/shard_map/ppermute | solution.py:452
  20.4 0.0 collective-permute-done
  20.4 1.1 %collective-permute-start.2 = (f32[36,128]{1,0:T(8,128)S(1)}, f32[36,128]{1,0:T(8,128)S(1)}, u32[]{:S(2)}, u32[]{:S(2)}) collective-permute-start(f32[36,128]{1,0:T(8,128)S(1)} %pad_maximum_fusion.refs_0_), channel_id=1, source_target_pairs={{0,4},{1,5},{2,6},{3,7},{4,0},{5,1},{6,2},{7,3},{8,12},{9,13},{10,... | collective-permute-start | bytes 55304 | tf_op jit(solution)/shard_map/ppermute | solution.py:452
  21.5 0.3 %collective-permute-start.1 = (f32[36,128]{1,0:T(8,128)S(1)}, f32[36,128]{1,0:T(8,128)S(1)}, u32[]{:S(2)}, u32[]{:S(2)}) collective-permute-start(f32[36,128]{1,0:T(8,128)S(1)} %pad_maximum_fusion.refs_0_), channel_id=1, source_target_pairs={{0,2},{1,3},{2,0},{3,1},{4,6},{5,7},{6,4},{7,5},{8,10},{9,11},{10,... | collective-permute-start | bytes 55304 | tf_op jit(solution)/shard_map/ppermute | solution.py:452
  21.8 0.0 collective-permute-done.3.refs_3_
  21.8 1.1 %collective-permute-start.4 = (f32[18,128]{1,0:T(8,128)S(1)}, f32[18,128]{1,0:T(8,128)S(1)}, u32[]{:S(2)}, u32[]{:S(2)}) collective-permute-start(f32[18,128]{1,0:T(8,128)S(1)} %collective-permute-done.3.refs_3_), channel_id=1, source_target_pairs={{0,1},{1,0},{2,3},{3,2},{4,5},{5,4},{6,7},{7,6},{8,9},{9,8},{10,11... | collective-permute-start | bytes 27656 | tf_op jit(solution)/shard_map/ppermute | solution.py:452
  22.9 0.8 %collective-permute-done.4.refs_4_ = f32[18,128]{1,0:T(8,128)S(1)} collective-permute-done((f32[18,128]{1,0:T(8,128)S(1)}, f32[18,128]{1,0:T(8,128)S(1)}, u32[]{:S(2)}, u32[]{:S(2)}) %collective-permute-start.4) | collective-permute-done | bytes 9248 | tf_op jit(solution)/shard_map/ppermute | solution.py:452
  23.7 0.9 %collective-permute-done.2.refs_2_ = f32[36,128]{1,0:T(8,128)S(1)} collective-permute-done((f32[36,128]{1,0:T(8,128)S(1)}, f32[36,128]{1,0:T(8,128)S(1)}, u32[]{:S(2)}, u32[]{:S(2)}) %collective-permute-start.2) | collective-permute-done | bytes 18464 | tf_op jit(solution)/shard_map/ppermute | solution.py:452
  24.6 0.0 collective-permute-done.1.refs_1_
  24.6 1.1 %y_join.1 = f32[1024,128]{1,0:T(8,128)} custom-call(f32[36,128]{1,0:T(8,128)S(1)} %pad_maximum_fusion.refs_0_, f32[36,128]{1,0:T(8,128)S(1)} %collective-permute-done.1.refs_1_, f32[36,128]{1,0:T(8,128)S(1)} %collective-permute-done.2.refs_2_, f32[18,128]{1,0:T(8,128)S(1)} %collective-permute-done.3.refs_3_, f32[18,128]{1,0:T(8,128)S(1)} %collective-permute-done.4.refs_4_, ...), custom_call_target="tpu_custom_call" | custom-call | tf_op jit(solution)/shard_map/y_join/pallas_call | solution.py:503
  (1 shorter events, 0.0 us)
Async XLA Ops:
  1.5 13.8 %copy-start = (f32[1,128,256]{2,1,0:T(8,128)S(1)}, f32[1,128,256]{2,1,0:T(8,128)}, u32[]{:S(2)}) copy-start(f32[1,128,256]{2,1,0:T(8,128)} %param.4) | copy-start | bytes 393220
  1.5 13.8 %copy-start.1 = (f32[1,128,256]{2,1,0:T(8,128)S(1)}, f32[1,128,256]{2,1,0:T(8,128)}, u32[]{:S(2)}) copy-start(f32[1,128,256]{2,1,0:T(8,128)} %param.5) | copy-start | bytes 393220
  16.2 4.2 %collective-permute-start = (f32[18,128]{1,0:T(8,128)S(1)}, f32[18,128]{1,0:T(8,128)S(1)}, u32[]{:S(2)}, u32[]{:S(2)}) collective-permute-start(f32[18,128]{1,0:T(8,128)S(1)} %get-tuple-element.14), channel_id=1, source_target_pairs={{0,1},{1,0},{2,3},{3,2},{4,5},{5,4},{6,7},{7,6},{8,9},{9,8},{10,11... | collective-permute-start | bytes 27656 | tf_op jit(solution)/shard_map/ppermute | solution.py:452
  17.9 3.9 %collective-permute-start.3 = (f32[18,128]{1,0:T(8,128)S(1)}, f32[18,128]{1,0:T(8,128)S(1)}, u32[]{:S(2)}, u32[]{:S(2)}) collective-permute-start(f32[18,128]{1,0:T(8,128)S(1)} %get-tuple-element.14), channel_id=1, source_target_pairs={{0,6},{1,7},{2,4},{3,5},{4,2},{5,3},{6,0},{7,1},{8,14},{9,15},{10,... | collective-permute-start | bytes 27656 | tf_op jit(solution)/shard_map/ppermute | solution.py:452
  20.4 4.2 %collective-permute-start.2 = (f32[36,128]{1,0:T(8,128)S(1)}, f32[36,128]{1,0:T(8,128)S(1)}, u32[]{:S(2)}, u32[]{:S(2)}) collective-permute-start(f32[36,128]{1,0:T(8,128)S(1)} %pad_maximum_fusion.refs_0_), channel_id=1, source_target_pairs={{0,4},{1,5},{2,6},{3,7},{4,0},{5,1},{6,2},{7,3},{8,12},{9,13},{10,... | collective-permute-start | bytes 55304 | tf_op jit(solution)/shard_map/ppermute | solution.py:452
  21.5 3.1 %collective-permute-start.1 = (f32[36,128]{1,0:T(8,128)S(1)}, f32[36,128]{1,0:T(8,128)S(1)}, u32[]{:S(2)}, u32[]{:S(2)}) collective-permute-start(f32[36,128]{1,0:T(8,128)S(1)} %pad_maximum_fusion.refs_0_), channel_id=1, source_target_pairs={{0,2},{1,3},{2,0},{3,1},{4,6},{5,7},{6,4},{7,5},{8,10},{9,11},{10,... | collective-permute-start | bytes 55304 | tf_op jit(solution)/shard_map/ppermute | solution.py:452
  21.8 1.9 %collective-permute-start.4 = (f32[18,128]{1,0:T(8,128)S(1)}, f32[18,128]{1,0:T(8,128)S(1)}, u32[]{:S(2)}, u32[]{:S(2)}) collective-permute-start(f32[18,128]{1,0:T(8,128)S(1)} %collective-permute-done.3.refs_3_), channel_id=1, source_target_pairs={{0,1},{1,0},{2,3},{3,2},{4,5},{5,4},{6,7},{7,6},{8,9},{9,8},{10,11... | collective-permute-start | bytes 27656 | tf_op jit(solution)/shard_map/ppermute | solution.py:452

commit v9 on v8

--- a/solution.py
+++ b/solution.py
@@ -301,8 +301,9 @@
 
 
 def place(parts, turned, ranks, rows, rank):
-    for k, other, message in parts:
-        chip = lax.bitwise_xor(lax.div(rank, 2), k)
+    mine = lax.div(rank, 2)
+    for chips, other, message in parts:
+        chip = sum(jnp.where(mine == i, source, 0) for i, source in enumerate(chips))
         device = 2 * chip + lax.bitwise_xor(lax.rem(rank, 2), int(other))
         at = lax.rem(device + ranks - rank - 1, ranks) * spaced(rows)
         turned[pl.ds(at, rows), :] = message
@@ -397,9 +398,9 @@
     count = blocks * LANES // SUB
     rank = lax.axis_index(axis)
     parts = []
-    for (k, others), ref in zip(layout, chips):
+    for (sources, others), ref in zip(layout, chips):
         for i, other in enumerate(others):
-            parts.append((k, other, ref[pl.ds(i * rows, rows), :]))
+            parts.append((sources, other, ref[pl.ds(i * rows, rows), :]))
     place(parts, turned, ranks, rows, rank)
     ends = solve_ring(received_rows(turned, ranks, rows, 1, 0), ranks, rank, half)
     copies = []
@@ -447,22 +448,28 @@
 X_ORDER = (10, 3, 1, 2, 0, 4, 5, 6, 7, 8, 9, 11, 12, 13, 14, 15)
 
 
+Y_ROUNDS = ((3, 2, 0, 1), (2, 3, 1, 0), (1, 0, 3, 2))
+
+
 def exchange_chips(message, ranks, axis):
-    def send(array, step):
-        return lax.ppermute(array, axis, [(i, i ^ step) for i in range(ranks)])
-
-    chips = range(1, ranks // 2)
-    early = chips[3 - 1]
-    near_chip = send(message, 2 * early)
-    other = send(message, 1)
-    both = jnp.concatenate([message, other])
-    layout, arrays = [(0, (False, True))], [both]
-    for k in chips:
-        if k != early:
-            layout.append((k, (False, True)))
-            arrays.append(send(both, 2 * k))
-    layout += [(early, (False,)), (early, (True,))]
-    arrays += [near_chip, send(near_chip, 1)]
+    def swap(array):
+        return lax.ppermute(array, axis, [(i, i ^ 1) for i in range(ranks)])
+
+    def send(array, to):
+        return lax.ppermute(array, axis, [(i, 2 * to[i // 2] + i % 2) for i in range(ranks)])
+
+    def sources(to):
+        return tuple(to.index(chip) for chip in range(len(to)))
+
+    first, *later = Y_ROUNDS
+    early = send(message, first)
+    both = jnp.concatenate([message, swap(message)])
+    layout, arrays = [(tuple(range(ranks // 2)), (False, True))], [both]
+    for to in reversed(later):
+        layout.append((sources(to), (False, True)))
+        arrays.append(send(both, to))
+    layout += [(sources(first), (False,)), (sources(first), (True,))]
+    arrays += [early, swap(early)]
     return layout, arrays
 
 

time: 26 us -> 25.8 us (level)
  waiting for transfers between devices: 1.73 us -> 1.14 us
  starting transfers between devices: 6.7 us -> 6.98 us
    ppermute x5, waiting for transfers between devices: 1.73 us -> 1.14 us  [the longest x2 0.84 us: swap(): return lax.ppermute(array, axis, [(i, i ^ 1) for i in range(ranks)])]
    ppermute x5, starting transfers between devices: 6.7 us -> 6.98 us  [the longest x3 4.26 us: send(): lax.ppermute(array, axis, [(i, 2 * to[i // 2] + i % 2) for i in range(ran...]
where the time goes in v9:
time: 25.8 us; the launch traced here: 25.5 us
  blocking collectives  13.8 us (53%)
  starting transfers between devices  6.98 us (27%)
  Pallas kernels  3.52 us (14%)
  waiting for transfers between devices  1.14 us (4%)
    all_to_all x1, blocking collectives, exchange(): lax.all_to_all(flat, axis, 0, 0, tiled=True, axis_index_groups=[list(orde...  13.8 us
    ppermute x3, starting transfers between devices, send(): lax.ppermute(array, axis, [(i, 2 * to[i // 2] + i % 2) for i in range(ran...  4.26 us
    ppermute x2, starting transfers between devices, swap(): return lax.ppermute(array, axis, [(i, i ^ 1) for i in range(ranks)])  2.72 us
    pallas_call x1, Pallas kernels, on_device(): call(functools.partial(x_ends_kernel, half_x, x_cells, blocks, x_ranks, x...  1.51 us
    pallas_call x1, Pallas kernels, on_device(): call(functools.partial(y_join_kernel, half_y, x_cells, blocks, 'gy', y_ra...  1.16 us
    pallas_call x1, Pallas kernels, on_device(): call(functools.partial(x_join_kernel, half_x, half_y, x_cells, blocks, 'g...  0.85 us
    ppermute x2, waiting for transfers between devices, swap(): return lax.ppermute(array, axis, [(i, i ^ 1) for i in range(ranks)])  0.84 us
  transfers between devices with their start and end apart: 5, of which 2 were waited for; matrix products, arithmetic and copies ran while one was open for 0% of the time, Pallas kernels for 0%

profile of v9, /device:TPU:1, one launch (start us, length us, event | category | flops | bytes accessed | tf_op | source)
XLA Modules:
  0.0 25.5 jit_solution(7345299599097163777)
XLA Ops:
  0.0 1.5 %x_ends.1 = (f32[576,128]{1,0:T(8,128)S(1)}, f32[2,2,320,128]{3,2,1,0:T(8,128)S(1)}, f32[4,2,160,128]{3,2,1,0:T(8,128)S(1)}) custom-call(f32[1024,128]{1,0:T(8,128)} %bitcast.28, f32[256,128]{1,0:T(8,128)} %bitcast.23, f32[256,128]{1,0:T(8,128)} %bitcast.25), custom_call_target="tpu_custom_call" | custom-call | tf_op jit(solution)/shard_map/x_ends/pallas_call | solution.py:488
  1.5 0.0 copy-start
  1.5 0.0 copy-start.1
  1.5 13.8 %all_to_all.5 = f32[16,1,4608]{2,1,0:T(1,128)S(1)} all-to-all(f32[16,1,4608]{2,1,0:T(1,128)S(1)} %bitcast.27), channel_id=1, replica_groups={{80,24,8,16,0,32,40,48,56,64,72,88,96,104,112,120},{81,25,9,17,1,33,41,..., dimensions={0} | all-to-all | bytes 589824 | tf_op jit(solution)/shard_map/all_to_all | solution.py:445
  15.3 0.0 copy-done
  15.3 0.0 copy-done.1
  15.3 0.9 %x_join.1 = (f32[18,128]{1,0:T(8,128)S(1)}, f32[2,576,128]{2,1,0:T(8,128)S(1)}, f32[4,288,128]{2,1,0:T(8,128)S(1)}) custom-call(f32[576,128]{1,0:T(8,128)S(1)} %bitcast.22, f32[2,2,320,128]{3,2,1,0:T(8,128)S(1)} %get-tuple-element.12.x_weights, f32[4,2,160,128]{3,2,1,0:T(8,128)S(1)} %get-tuple-element.13.x_pushed, f32[256,128]{1,0:T(8,128)S(1)} %bitcast.24, ...), custom_call_target="tpu_custom_call" | custom-call | tf_op jit(solution)/shard_map/x_join/pallas_call | solution.py:499
  16.2 1.7 %collective-permute-start = (f32[18,128]{1,0:T(8,128)S(1)}, f32[18,128]{1,0:T(8,128)S(1)}, u32[]{:S(2)}, u32[]{:S(2)}) collective-permute-start(f32[18,128]{1,0:T(8,128)S(1)} %get-tuple-element.14), channel_id=1, source_target_pairs={{0,1},{1,0},{2,3},{3,2},{4,5},{5,4},{6,7},{7,6},{8,9},{9,8},{10,11... | collective-permute-start | bytes 27656 | tf_op jit(solution)/shard_map/ppermute | solution.py:456
  17.9 2.5 %collective-permute-start.3 = (f32[18,128]{1,0:T(8,128)S(1)}, f32[18,128]{1,0:T(8,128)S(1)}, u32[]{:S(2)}, u32[]{:S(2)}) collective-permute-start(f32[18,128]{1,0:T(8,128)S(1)} %get-tuple-element.14), channel_id=1, source_target_pairs={{0,6},{1,7},{2,4},{3,5},{4,0},{5,1},{6,2},{7,3},{8,14},{9,15},{10,... | collective-permute-start | bytes 27656 | tf_op jit(solution)/shard_map/ppermute | solution.py:459
  20.4 0.0 collective-permute-done
  20.4 1.1 %collective-permute-start.2 = (f32[36,128]{1,0:T(8,128)S(1)}, f32[36,128]{1,0:T(8,128)S(1)}, u32[]{:S(2)}, u32[]{:S(2)}) collective-permute-start(f32[36,128]{1,0:T(8,128)S(1)} %pad_maximum_fusion.refs_0_), channel_id=1, source_target_pairs={{0,4},{1,5},{2,6},{3,7},{4,2},{5,3},{6,0},{7,1},{8,12},{9,13},{10,... | collective-permute-start | bytes 55304 | tf_op jit(solution)/shard_map/ppermute | solution.py:459
  21.5 0.7 %collective-permute-start.1 = (f32[36,128]{1,0:T(8,128)S(1)}, f32[36,128]{1,0:T(8,128)S(1)}, u32[]{:S(2)}, u32[]{:S(2)}) collective-permute-start(f32[36,128]{1,0:T(8,128)S(1)} %pad_maximum_fusion.refs_0_), channel_id=1, source_target_pairs={{0,2},{1,3},{2,0},{3,1},{4,6},{5,7},{6,4},{7,5},{8,10},{9,11},{10,... | collective-permute-start | bytes 55304 | tf_op jit(solution)/shard_map/ppermute | solution.py:459
  22.2 0.0 collective-permute-done.3.refs_3_
  22.2 1.0 %collective-permute-start.4 = (f32[18,128]{1,0:T(8,128)S(1)}, f32[18,128]{1,0:T(8,128)S(1)}, u32[]{:S(2)}, u32[]{:S(2)}) collective-permute-start(f32[18,128]{1,0:T(8,128)S(1)} %collective-permute-done.3.refs_3_), channel_id=1, source_target_pairs={{0,1},{1,0},{2,3},{3,2},{4,5},{5,4},{6,7},{7,6},{8,9},{9,8},{10,11... | collective-permute-start | bytes 27656 | tf_op jit(solution)/shard_map/ppermute | solution.py:456
  23.2 0.8 %collective-permute-done.4.refs_4_ = f32[18,128]{1,0:T(8,128)S(1)} collective-permute-done((f32[18,128]{1,0:T(8,128)S(1)}, f32[18,128]{1,0:T(8,128)S(1)}, u32[]{:S(2)}, u32[]{:S(2)}) %collective-permute-start.4) | collective-permute-done | bytes 9248 | tf_op jit(solution)/shard_map/ppermute | solution.py:456
  24.0 0.3 %collective-permute-done.2.refs_2_ = f32[36,128]{1,0:T(8,128)S(1)} collective-permute-done((f32[36,128]{1,0:T(8,128)S(1)}, f32[36,128]{1,0:T(8,128)S(1)}, u32[]{:S(2)}, u32[]{:S(2)}) %collective-permute-start.2) | collective-permute-done | bytes 18464 | tf_op jit(solution)/shard_map/ppermute | solution.py:459
  24.3 0.0 collective-permute-done.1.refs_1_
  24.3 1.2 %y_join.1 = f32[1024,128]{1,0:T(8,128)} custom-call(f32[36,128]{1,0:T(8,128)S(1)} %pad_maximum_fusion.refs_0_, f32[36,128]{1,0:T(8,128)S(1)} %collective-permute-done.1.refs_1_, f32[36,128]{1,0:T(8,128)S(1)} %collective-permute-done.2.refs_2_, f32[18,128]{1,0:T(8,128)S(1)} %collective-permute-done.3.refs_3_, f32[18,128]{1,0:T(8,128)S(1)} %collective-permute-done.4.refs_4_, ...), custom_call_target="tpu_custom_call" | custom-call | tf_op jit(solution)/shard_map/y_join/pallas_call | solution.py:510
  (1 shorter events, 0.0 us)
Async XLA Ops:
  1.5 13.8 %copy-start = (f32[1,128,256]{2,1,0:T(8,128)S(1)}, f32[1,128,256]{2,1,0:T(8,128)}, u32[]{:S(2)}) copy-start(f32[1,128,256]{2,1,0:T(8,128)} %param.4) | copy-start | bytes 393220
  1.5 13.8 %copy-start.1 = (f32[1,128,256]{2,1,0:T(8,128)S(1)}, f32[1,128,256]{2,1,0:T(8,128)}, u32[]{:S(2)}) copy-start(f32[1,128,256]{2,1,0:T(8,128)} %param.5) | copy-start | bytes 393220
  16.2 4.2 %collective-permute-start = (f32[18,128]{1,0:T(8,128)S(1)}, f32[18,128]{1,0:T(8,128)S(1)}, u32[]{:S(2)}, u32[]{:S(2)}) collective-permute-start(f32[18,128]{1,0:T(8,128)S(1)} %get-tuple-element.14), channel_id=1, source_target_pairs={{0,1},{1,0},{2,3},{3,2},{4,5},{5,4},{6,7},{7,6},{8,9},{9,8},{10,11... | collective-permute-start | bytes 27656 | tf_op jit(solution)/shard_map/ppermute | solution.py:456
  17.9 4.3 %collective-permute-start.3 = (f32[18,128]{1,0:T(8,128)S(1)}, f32[18,128]{1,0:T(8,128)S(1)}, u32[]{:S(2)}, u32[]{:S(2)}) collective-permute-start(f32[18,128]{1,0:T(8,128)S(1)} %get-tuple-element.14), channel_id=1, source_target_pairs={{0,6},{1,7},{2,4},{3,5},{4,0},{5,1},{6,2},{7,3},{8,14},{9,15},{10,... | collective-permute-start | bytes 27656 | tf_op jit(solution)/shard_map/ppermute | solution.py:459
  20.4 3.9 %collective-permute-start.2 = (f32[36,128]{1,0:T(8,128)S(1)}, f32[36,128]{1,0:T(8,128)S(1)}, u32[]{:S(2)}, u32[]{:S(2)}) collective-permute-start(f32[36,128]{1,0:T(8,128)S(1)} %pad_maximum_fusion.refs_0_), channel_id=1, source_target_pairs={{0,4},{1,5},{2,6},{3,7},{4,2},{5,3},{6,0},{7,1},{8,12},{9,13},{10,... | collective-permute-start | bytes 55304 | tf_op jit(solution)/shard_map/ppermute | solution.py:459
  21.5 2.8 %collective-permute-start.1 = (f32[36,128]{1,0:T(8,128)S(1)}, f32[36,128]{1,0:T(8,128)S(1)}, u32[]{:S(2)}, u32[]{:S(2)}) collective-permute-start(f32[36,128]{1,0:T(8,128)S(1)} %pad_maximum_fusion.refs_0_), channel_id=1, source_target_pairs={{0,2},{1,3},{2,0},{3,1},{4,6},{5,7},{6,4},{7,5},{8,10},{9,11},{10,... | collective-permute-start | bytes 55304 | tf_op jit(solution)/shard_map/ppermute | solution.py:459
  22.2 1.8 %collective-permute-start.4 = (f32[18,128]{1,0:T(8,128)S(1)}, f32[18,128]{1,0:T(8,128)S(1)}, u32[]{:S(2)}, u32[]{:S(2)}) collective-permute-start(f32[18,128]{1,0:T(8,128)S(1)} %collective-permute-done.3.refs_3_), channel_id=1, source_target_pairs={{0,1},{1,0},{2,3},{3,2},{4,5},{5,4},{6,7},{7,6},{8,9},{9,8},{10,11... | collective-permute-start | bytes 27656 | tf_op jit(solution)/shard_map/ppermute | solution.py:456

commit v10 on v9

--- a/solution.py
+++ b/solution.py
@@ -414,9 +414,11 @@
             value = lines[block * LANES : (block + 1) * LANES].T
             for i in range(x_cells // SUB):
                 here[pl.ds(tile_at(f, i, block, x_cells, blocks), SUB), :] = value[i * SUB : (i + 1) * SUB]
-        part = pl.ds(f * per_field, per_field)
-        copies.append(pltpu.make_async_copy(here.at[part], updated.at[part], left.at[f]))
-        copies[-1].start()
+        for low, high in ((0, 0), (1, 2), (3, 3)):
+            if f == high:
+                part = pl.ds(low * per_field, (high + 1 - low) * per_field)
+                copies.append(pltpu.make_async_copy(here.at[part], updated.at[part], left.at[f]))
+                copies[-1].start()
     for copy in copies:
         copy.wait()
 

time: 25.8 us -> 25.8 us (level)
  no operation moved by 1% of the time
where the time goes in v10:
time: 25.8 us; the launch traced here: 25.5 us
  blocking collectives  13.8 us (53%)
  starting transfers between devices  6.98 us (27%)
  Pallas kernels  3.52 us (14%)
  waiting for transfers between devices  1.14 us (4%)
    all_to_all x1, blocking collectives, exchange(): lax.all_to_all(flat, axis, 0, 0, tiled=True, axis_index_groups=[list(orde...  13.8 us
    ppermute x3, starting transfers between devices, send(): lax.ppermute(array, axis, [(i, 2 * to[i // 2] + i % 2) for i in range(ran...  4.26 us
    ppermute x2, starting transfers between devices, swap(): return lax.ppermute(array, axis, [(i, i ^ 1) for i in range(ranks)])  2.72 us
    pallas_call x1, Pallas kernels, on_device(): call(functools.partial(x_ends_kernel, half_x, x_cells, blocks, x_ranks, x...  1.51 us
    pallas_call x1, Pallas kernels, on_device(): call(functools.partial(y_join_kernel, half_y, x_cells, blocks, 'gy', y_ra...  1.16 us
    pallas_call x1, Pallas kernels, on_device(): call(functools.partial(x_join_kernel, half_x, half_y, x_cells, blocks, 'g...  0.85 us
    ppermute x2, waiting for transfers between devices, swap(): return lax.ppermute(array, axis, [(i, i ^ 1) for i in range(ranks)])  0.84 us
  transfers between devices with their start and end apart: 5, of which 2 were waited for; matrix products, arithmetic and copies ran while one was open for 0% of the time, Pallas kernels for 0%

profile of v10, /device:TPU:1, one launch (start us, length us, event | category | flops | bytes accessed | tf_op | source)
XLA Modules:
  0.0 25.5 jit_solution(8412998175771118576)
XLA Ops:
  0.0 1.5 %x_ends.1 = (f32[576,128]{1,0:T(8,128)S(1)}, f32[2,2,320,128]{3,2,1,0:T(8,128)S(1)}, f32[4,2,160,128]{3,2,1,0:T(8,128)S(1)}) custom-call(f32[1024,128]{1,0:T(8,128)} %bitcast.28, f32[256,128]{1,0:T(8,128)} %bitcast.23, f32[256,128]{1,0:T(8,128)} %bitcast.25), custom_call_target="tpu_custom_call" | custom-call | tf_op jit(solution)/shard_map/x_ends/pallas_call | solution.py:490
  1.5 0.0 copy-start
  1.5 0.0 copy-start.1
  1.5 13.8 %all_to_all.5 = f32[16,1,4608]{2,1,0:T(1,128)S(1)} all-to-all(f32[16,1,4608]{2,1,0:T(1,128)S(1)} %bitcast.27), channel_id=1, replica_groups={{80,24,8,16,0,32,40,48,56,64,72,88,96,104,112,120},{81,25,9,17,1,33,41,..., dimensions={0} | all-to-all | bytes 589824 | tf_op jit(solution)/shard_map/all_to_all | solution.py:447
  15.3 0.0 copy-done
  15.3 0.0 copy-done.1
  15.3 0.9 %x_join.1 = (f32[18,128]{1,0:T(8,128)S(1)}, f32[2,576,128]{2,1,0:T(8,128)S(1)}, f32[4,288,128]{2,1,0:T(8,128)S(1)}) custom-call(f32[576,128]{1,0:T(8,128)S(1)} %bitcast.22, f32[2,2,320,128]{3,2,1,0:T(8,128)S(1)} %get-tuple-element.12.x_weights, f32[4,2,160,128]{3,2,1,0:T(8,128)S(1)} %get-tuple-element.13.x_pushed, f32[256,128]{1,0:T(8,128)S(1)} %bitcast.24, ...), custom_call_target="tpu_custom_call" | custom-call | tf_op jit(solution)/shard_map/x_join/pallas_call | solution.py:501
  16.2 1.7 %collective-permute-start = (f32[18,128]{1,0:T(8,128)S(1)}, f32[18,128]{1,0:T(8,128)S(1)}, u32[]{:S(2)}, u32[]{:S(2)}) collective-permute-start(f32[18,128]{1,0:T(8,128)S(1)} %get-tuple-element.14), channel_id=1, source_target_pairs={{0,1},{1,0},{2,3},{3,2},{4,5},{5,4},{6,7},{7,6},{8,9},{9,8},{10,11... | collective-permute-start | bytes 27656 | tf_op jit(solution)/shard_map/ppermute | solution.py:458
  17.9 2.5 %collective-permute-start.3 = (f32[18,128]{1,0:T(8,128)S(1)}, f32[18,128]{1,0:T(8,128)S(1)}, u32[]{:S(2)}, u32[]{:S(2)}) collective-permute-start(f32[18,128]{1,0:T(8,128)S(1)} %get-tuple-element.14), channel_id=1, source_target_pairs={{0,6},{1,7},{2,4},{3,5},{4,0},{5,1},{6,2},{7,3},{8,14},{9,15},{10,... | collective-permute-start | bytes 27656 | tf_op jit(solution)/shard_map/ppermute | solution.py:461
  20.4 0.0 collective-permute-done
  20.4 1.1 %collective-permute-start.2 = (f32[36,128]{1,0:T(8,128)S(1)}, f32[36,128]{1,0:T(8,128)S(1)}, u32[]{:S(2)}, u32[]{:S(2)}) collective-permute-start(f32[36,128]{1,0:T(8,128)S(1)} %pad_maximum_fusion.refs_0_), channel_id=1, source_target_pairs={{0,4},{1,5},{2,6},{3,7},{4,2},{5,3},{6,0},{7,1},{8,12},{9,13},{10,... | collective-permute-start | bytes 55304 | tf_op jit(solution)/shard_map/ppermute | solution.py:461
  21.5 0.7 %collective-permute-start.1 = (f32[36,128]{1,0:T(8,128)S(1)}, f32[36,128]{1,0:T(8,128)S(1)}, u32[]{:S(2)}, u32[]{:S(2)}) collective-permute-start(f32[36,128]{1,0:T(8,128)S(1)} %pad_maximum_fusion.refs_0_), channel_id=1, source_target_pairs={{0,2},{1,3},{2,0},{3,1},{4,6},{5,7},{6,4},{7,5},{8,10},{9,11},{10,... | collective-permute-start | bytes 55304 | tf_op jit(solution)/shard_map/ppermute | solution.py:461
  22.2 0.0 collective-permute-done.3.refs_3_
  22.2 1.0 %collective-permute-start.4 = (f32[18,128]{1,0:T(8,128)S(1)}, f32[18,128]{1,0:T(8,128)S(1)}, u32[]{:S(2)}, u32[]{:S(2)}) collective-permute-start(f32[18,128]{1,0:T(8,128)S(1)} %collective-permute-done.3.refs_3_), channel_id=1, source_target_pairs={{0,1},{1,0},{2,3},{3,2},{4,5},{5,4},{6,7},{7,6},{8,9},{9,8},{10,11... | collective-permute-start | bytes 27656 | tf_op jit(solution)/shard_map/ppermute | solution.py:458
  23.2 0.8 %collective-permute-done.4.refs_4_ = f32[18,128]{1,0:T(8,128)S(1)} collective-permute-done((f32[18,128]{1,0:T(8,128)S(1)}, f32[18,128]{1,0:T(8,128)S(1)}, u32[]{:S(2)}, u32[]{:S(2)}) %collective-permute-start.4) | collective-permute-done | bytes 9248 | tf_op jit(solution)/shard_map/ppermute | solution.py:458
  24.0 0.3 %collective-permute-done.2.refs_2_ = f32[36,128]{1,0:T(8,128)S(1)} collective-permute-done((f32[36,128]{1,0:T(8,128)S(1)}, f32[36,128]{1,0:T(8,128)S(1)}, u32[]{:S(2)}, u32[]{:S(2)}) %collective-permute-start.2) | collective-permute-done | bytes 18464 | tf_op jit(solution)/shard_map/ppermute | solution.py:461
  24.3 0.0 collective-permute-done.1.refs_1_
  24.3 1.2 %y_join.1 = f32[1024,128]{1,0:T(8,128)} custom-call(f32[36,128]{1,0:T(8,128)S(1)} %pad_maximum_fusion.refs_0_, f32[36,128]{1,0:T(8,128)S(1)} %collective-permute-done.1.refs_1_, f32[36,128]{1,0:T(8,128)S(1)} %collective-permute-done.2.refs_2_, f32[18,128]{1,0:T(8,128)S(1)} %collective-permute-done.3.refs_3_, f32[18,128]{1,0:T(8,128)S(1)} %collective-permute-done.4.refs_4_, ...), custom_call_target="tpu_custom_call" | custom-call | tf_op jit(solution)/shard_map/y_join/pallas_call | solution.py:512
  (1 shorter events, 0.0 us)
Async XLA Ops:
  1.5 13.8 %copy-start = (f32[1,128,256]{2,1,0:T(8,128)S(1)}, f32[1,128,256]{2,1,0:T(8,128)}, u32[]{:S(2)}) copy-start(f32[1,128,256]{2,1,0:T(8,128)} %param.4) | copy-start | bytes 393220
  1.5 13.8 %copy-start.1 = (f32[1,128,256]{2,1,0:T(8,128)S(1)}, f32[1,128,256]{2,1,0:T(8,128)}, u32[]{:S(2)}) copy-start(f32[1,128,256]{2,1,0:T(8,128)} %param.5) | copy-start | bytes 393220
  16.2 4.2 %collective-permute-start = (f32[18,128]{1,0:T(8,128)S(1)}, f32[18,128]{1,0:T(8,128)S(1)}, u32[]{:S(2)}, u32[]{:S(2)}) collective-permute-start(f32[18,128]{1,0:T(8,128)S(1)} %get-tuple-element.14), channel_id=1, source_target_pairs={{0,1},{1,0},{2,3},{3,2},{4,5},{5,4},{6,7},{7,6},{8,9},{9,8},{10,11... | collective-permute-start | bytes 27656 | tf_op jit(solution)/shard_map/ppermute | solution.py:458
  17.9 4.3 %collective-permute-start.3 = (f32[18,128]{1,0:T(8,128)S(1)}, f32[18,128]{1,0:T(8,128)S(1)}, u32[]{:S(2)}, u32[]{:S(2)}) collective-permute-start(f32[18,128]{1,0:T(8,128)S(1)} %get-tuple-element.14), channel_id=1, source_target_pairs={{0,6},{1,7},{2,4},{3,5},{4,0},{5,1},{6,2},{7,3},{8,14},{9,15},{10,... | collective-permute-start | bytes 27656 | tf_op jit(solution)/shard_map/ppermute | solution.py:461
  20.4 3.9 %collective-permute-start.2 = (f32[36,128]{1,0:T(8,128)S(1)}, f32[36,128]{1,0:T(8,128)S(1)}, u32[]{:S(2)}, u32[]{:S(2)}) collective-permute-start(f32[36,128]{1,0:T(8,128)S(1)} %pad_maximum_fusion.refs_0_), channel_id=1, source_target_pairs={{0,4},{1,5},{2,6},{3,7},{4,2},{5,3},{6,0},{7,1},{8,12},{9,13},{10,... | collective-permute-start | bytes 55304 | tf_op jit(solution)/shard_map/ppermute | solution.py:461
  21.5 2.8 %collective-permute-start.1 = (f32[36,128]{1,0:T(8,128)S(1)}, f32[36,128]{1,0:T(8,128)S(1)}, u32[]{:S(2)}, u32[]{:S(2)}) collective-permute-start(f32[36,128]{1,0:T(8,128)S(1)} %pad_maximum_fusion.refs_0_), channel_id=1, source_target_pairs={{0,2},{1,3},{2,0},{3,1},{4,6},{5,7},{6,4},{7,5},{8,10},{9,11},{10,... | collective-permute-start | bytes 55304 | tf_op jit(solution)/shard_map/ppermute | solution.py:461
  22.2 1.8 %collective-permute-start.4 = (f32[18,128]{1,0:T(8,128)S(1)}, f32[18,128]{1,0:T(8,128)S(1)}, u32[]{:S(2)}, u32[]{:S(2)}) collective-permute-start(f32[18,128]{1,0:T(8,128)S(1)} %collective-permute-done.3.refs_3_), channel_id=1, source_target_pairs={{0,1},{1,0},{2,3},{3,2},{4,5},{5,4},{6,7},{7,6},{8,9},{9,8},{10,11... | collective-permute-start | bytes 27656 | tf_op jit(solution)/shard_map/ppermute | solution.py:458
